TPU v7x, 256 devices: a whole 4x4x8 slice. The times are simulated.
256 devices in a mesh: region: 32 (over z, y), tm: 8 (over x, core).
Axes of the slice: x: 4, y: 4, z: 8, core: 2. Of those that a mesh axis runs over, the one named last changes fastest.
Arguments:
- signal: bfloat16 [32, 32, 131072], P('tm', None, 'region'), may hold values from -6 to 6
- time_weight: bfloat16 [2, 64, 32], replicated, may hold values from -0.75 to 0.75
- time_bias: float32 [64], replicated, may hold values from -3 to 3
- mix_weight: bfloat16 [32, 160], replicated, may hold values from -1 to 1
- mix_bias: float32 [32], replicated, may hold values from -3 to 3
- tile_values: bfloat16 [32, 96, 128, 128], P('region'), may hold values from -1 to 1
- tile_rows: int32 [32, 96], P('region'), may hold values from 0 to 31, as said below
- tile_cols: int32 [32, 96], P('region'), may hold values from 0 to 39, as said below
- tile_count: int32 [32], P('region'), may hold values from 34 to 96, as said below
Outputs:
- layer_out: bfloat16 [32, 32, 131072], P('tm', None, 'region')
Inputs may be any that keep to these rules, and one draw needn't show every extreme that they name: `tile_count`: some region has all 96 slots live in every draw. `tile_rows`: slot s < 32 holds row tile s. `tile_cols`: values under 4 name the previous region's last 4 tiles, values of 36 or more the next region's first 4 tiles; the first region never names the previous one, the last never the next one. Slot s < 32 names s + 4.
All inputs are finite; a program needn't handle non-finite values.
Results may differ from a plain program's by a relative error of at most 0.0045.
Values may be sent and summed in bfloat16 or wider, within the bound.
A program may use at most 192 MiB of HBM per device.

v0:
```python
import jax
import jax.numpy as jnp
from jax import lax
from jax.sharding import PartitionSpec as P

DILATION_DAYS = 4
HB = 4


def padded(cells, sides, width):
    for axis, dim in sides:
        count = lax.axis_size(axis)
        ends = count - 1
        head = lax.slice_in_dim(cells, 0, width, axis=dim)
        tail = lax.slice_in_dim(cells, cells.shape[dim] - width, cells.shape[dim], axis=dim)
        cells = jnp.concatenate(
            [
                lax.ppermute(tail, axis, [(i, (i + 1) % count) for i in range(ends)]),
                cells,
                lax.ppermute(head, axis, [((i + 1) % count, i) for i in range(ends)]),
            ],
            axis=dim,
        )
    return cells


def shifted(shard, axis, by):
    size = lax.axis_size(axis)
    pairs = [(i, i + by) for i in range(size) if 0 <= i + by < size]
    return lax.ppermute(shard, axis, pairs)


def tile_apply(source, values, take_index, put_index, live_count, put_tiles, transposed):
    row_total = source.shape[0]
    source_tiles = source.shape[1]
    tile_size = values.shape[1]
    group_size = values.shape[0] // 3
    equation = "mgi,gij->mgj" if transposed else "mgj,gij->mgi"
    offsets = jnp.arange(group_size, dtype=jnp.int32)
    source_ids = jnp.arange(source_tiles, dtype=jnp.int32)
    target_ids = jnp.arange(put_tiles, dtype=jnp.int32)

    def add_block(turn_index, running):
        first_slot = turn_index * group_size
        block_values = lax.dynamic_slice_in_dim(values, first_slot, group_size, 0)
        block_take = lax.dynamic_slice_in_dim(take_index, first_slot, group_size, 0)
        block_put = lax.dynamic_slice_in_dim(put_index, first_slot, group_size, 0)
        live_slots = first_slot + offsets < live_count
        selector = (block_take[:, None] == source_ids[None, :]).astype(jnp.bfloat16)
        panels = jnp.einsum(
            "gt,mti->mgi", selector, source, preferred_element_type=jnp.float32
        ).astype(jnp.bfloat16)
        products = jnp.einsum(equation, panels, block_values, preferred_element_type=jnp.float32)
        placer = ((block_put[:, None] == target_ids[None, :]) & live_slots[:, None]).astype(
            jnp.float32
        )
        placed = jnp.einsum(
            "gp,mgj->mpj",
            placer,
            products,
            precision=lax.Precision.HIGHEST,
            preferred_element_type=jnp.float32,
        )
        return running + placed

    zero_sum = jnp.zeros((row_total, put_tiles, tile_size), jnp.float32)
    turn_count = 3
    return lax.fori_loop(0, turn_count, add_block, zero_sum)


def forward_hop(flattened, values, tile_rows, tile_cols, live_count):
    row_total, parcel_count = flattened.shape
    tile_size = values.shape[1]
    row_tiles = parcel_count // tile_size
    extended = padded(flattened, (("region", 1),), HB * tile_size)
    source = extended.reshape(row_total, row_tiles + 2 * HB, tile_size)
    running = tile_apply(source, values, tile_cols, tile_rows, live_count, row_tiles, False)
    return running.reshape(row_total, parcel_count).astype(jnp.bfloat16)


def backward_hop(flattened, values, tile_rows, tile_cols, live_count):
    row_total, parcel_count = flattened.shape
    tile_size = values.shape[1]
    row_tiles = parcel_count // tile_size
    source = flattened.reshape(row_total, row_tiles, tile_size)
    running = tile_apply(source, values, tile_rows, tile_cols, live_count, row_tiles + 2 * HB, True)
    lower_rim = running[:, :HB]
    middle = running[:, HB : HB + row_tiles]
    upper_rim = running[:, HB + row_tiles :]
    from_below = shifted(upper_rim.astype(jnp.bfloat16), "region", 1).astype(upper_rim.dtype)
    from_above = shifted(lower_rim.astype(jnp.bfloat16), "region", -1).astype(lower_rim.dtype)
    inner = middle[:, HB : row_tiles - HB]
    middle = jnp.concatenate(
        [middle[:, :HB] + from_below, inner, middle[:, row_tiles - HB :] + from_above], 1
    )
    return middle.reshape(row_total, parcel_count).astype(jnp.bfloat16)


def gated_days(signal, time_weight, time_bias):
    count_of_days = signal.shape[0]
    channel_count = time_weight.shape[2]
    earlier_days = shifted(signal, "tm", 1)
    lagged_signal = jnp.concatenate([earlier_days, signal[: count_of_days - DILATION_DAYS]], 0)
    preact = jnp.einsum(
        "oc,dcn->don", time_weight[0], lagged_signal, preferred_element_type=jnp.float32
    )
    preact = preact + jnp.einsum(
        "oc,dcn->don", time_weight[1], signal, preferred_element_type=jnp.float32
    )
    preact = preact + time_bias[None, :, None]
    return (jnp.tanh(preact[:, :channel_count]) * jax.nn.sigmoid(preact[:, channel_count:])).astype(
        jnp.bfloat16
    )


def body(
    signal,
    time_weight,
    time_bias,
    mix_weight,
    mix_bias,
    tile_values,
    tile_rows,
    tile_cols,
    tile_count,
):
    count_of_days, channel_count, parcel_count = signal.shape
    hidden = gated_days(signal, time_weight, time_bias)
    flattened = hidden.reshape(count_of_days * channel_count, parcel_count)
    values = tile_values[0]
    rows_here = tile_rows[0]
    cols_here = tile_cols[0]
    live_count = tile_count[0]
    fwd_one = forward_hop(flattened, values, rows_here, cols_here, live_count)
    bwd_one = backward_hop(flattened, values, rows_here, cols_here, live_count)
    fwd_two = forward_hop(fwd_one, values, rows_here, cols_here, live_count)
    bwd_two = backward_hop(bwd_one, values, rows_here, cols_here, live_count)
    shape = (count_of_days, channel_count, parcel_count)
    branches = (
        hidden,
        fwd_one.reshape(shape),
        fwd_two.reshape(shape),
        bwd_one.reshape(shape),
        bwd_two.reshape(shape),
    )
    running = signal.astype(jnp.float32) + mix_bias[None, :, None]
    for branch_index in range(5):
        weight_part = mix_weight[
            :, branch_index * channel_count : (branch_index + 1) * channel_count
        ]
        running = running + jnp.einsum(
            "oc,dcn->don", weight_part, branches[branch_index], preferred_element_type=jnp.float32
        )
    return running.astype(jnp.bfloat16)


def solution(mesh):
    placed = (
        P("tm", None, "region"),
        P(),
        P(),
        P(),
        P(),
        P("region", None, None, None),
        P("region", None),
        P("region", None),
        P("region"),
    )
    return jax.shard_map(
        body, mesh=mesh, in_specs=placed, out_specs=P("tm", None, "region"), check_vma=False
    )
```

profile of v0, /device:TPU:126, one launch (start us, length us, event | category | flops | bytes accessed | tf_op | source)
XLA Modules:
  0.0 226.4 jit_solution(4496903222186596303)
XLA Ops:
  4.0 12.3 %collective-permute-done = bf16[4,32,4096]{2,1,0:T(8,128)(2,1)S(1)} collective-permute-done((bf16[4,32,4096]{2,1,0:T(8,128)(2,1)}, bf16[4,32,4096]{2,1,0:T(8,128)(2,1)S(1)}, u32[]{:S(2)}, u32[]{:S(2)}) %collective-permute-start) | collective-permute-done | bytes 1048608 | tf_op jit(solution)/shard_map/ppermute | solution.py:30
  19.4 35.7 %while.66 = (s32[]{:T(128)}, f32[128,40,128]{2,1,0:T(8,128)}, bf16[96,128,128]{2,1,0:T(8,128)(2,1)}, s32[96]{0:T(128)}, bf16[128,32,128]{2,1,0:T(8,128)(2,1)S(1)...) while((s32[]{:T(128)}, f32[128,40,128]{2,1,0:T(8,128)}, ...), condition=%wide.region_5.0_spmd.clone.clone, body=%wide.region_4.0_spmd.clone.clone.sunk | while | flops 420744768 | bytes 17826816 | solution.py:68
  26.2 4.6 %bitcast_add_fusion.10 = f32[128,40,128]{2,1,0:T(8,128)} fusion(f32[128,40,128]{2,1,0:T(8,128)} %get-tuple-element.1259, f32[32,128,128]{1,0,2:T(8,128)} %copy.53, pred[]{:T(512)S(6)} %compare.14, s32[32]{0:T(128)S(1)} %dynamic_slice.148, pred[32]{0:T(512)(128)(4,1)S(1)} %fusion.197), kind=kOutput, calls=%fused_computation.46.clone.1 | convolution fusion | flops 252971520 | bytes 7340193 | tf_op jit(solution)/shard_map/while/body/eval_jaxpr/gp,mgj->mpj/dot_general | solution.py:57
  37.6 5.3 %bitcast_add_fusion.10 = f32[128,40,128]{2,1,0:T(8,128)} fusion(f32[128,40,128]{2,1,0:T(8,128)} %get-tuple-element.1259, f32[32,128,128]{1,0,2:T(8,128)} %copy.53, pred[]{:T(512)S(6)} %compare.14, s32[32]{0:T(128)S(1)} %dynamic_slice.148, pred[32]{0:T(512)(128)(4,1)S(1)} %fusion.197), kind=kOutput, calls=%fused_computation.46.clone.1 | convolution fusion | flops 252971520 | bytes 7340193 | tf_op jit(solution)/shard_map/while/body/eval_jaxpr/gp,mgj->mpj/dot_general | solution.py:57
  49.7 5.3 %bitcast_add_fusion.10 = f32[128,40,128]{2,1,0:T(8,128)} fusion(f32[128,40,128]{2,1,0:T(8,128)} %get-tuple-element.1259, f32[32,128,128]{1,0,2:T(8,128)} %copy.53, pred[]{:T(512)S(6)} %compare.14, s32[32]{0:T(128)S(1)} %dynamic_slice.148, pred[32]{0:T(512)(128)(4,1)S(1)} %fusion.197), kind=kOutput, calls=%fused_computation.46.clone.1 | convolution fusion | flops 252971520 | bytes 7340193 | tf_op jit(solution)/shard_map/while/body/eval_jaxpr/gp,mgj->mpj/dot_general | solution.py:57
  62.3 6.5 %collective-permute-start.1 = (bf16[128,512]{1,0:T(8,128)(2,1)S(1)}, bf16[128,512]{1,0:T(8,128)(2,1)S(1)}, u32[]{:S(2)}, u32[]{:S(2)}) collective-permute-start(bf16[128,512]{1,0:T(8,128)(2,1)S(1)} %get-tuple-element.1007), channel_id=1, source_target_pairs={{0,8},{8,16},{16,24},{24,32},{32,40},{40,48},{48,56},{56,64},{64,7... | collective-permute-start | bytes 393224 | tf_op jit(solution)/shard_map/ppermute | solution.py:18
  71.5 3.9 %collective-permute-start.6 = (bf16[128,4,128]{2,1,0:T(4,128)(2,1)}, bf16[128,4,128]{2,1,0:T(4,128)(2,1)}, u32[]{:S(2)}, u32[]{:S(2)}) collective-permute-start(bf16[128,4,128]{2,1,0:T(4,128)(2,1)} %get-tuple-element.1004), channel_id=1, source_target_pairs={{8,0},{16,8},{24,16},{32,24},{40,32},{48,40},{56,48},{64,56},{72,6... | collective-permute-start | bytes 393224 | tf_op jit(solution)/shard_map/ppermute | solution.py:30
  77.7 36.4 %while.64 = (s32[]{:T(128)}, f32[128,32,128]{2,1,0:T(8,128)}, bf16[96,128,128]{2,1,0:T(8,128)(2,1)}, s32[96]{0:T(128)}, bf16[128,40,128]{2,1,0:T(8,128)(2,1)S(1)...) while((s32[]{:T(128)}, f32[128,32,128]{2,1,0:T(8,128)}, ...), condition=%wide.region_1.0_spmd.clone.clone, body=%wide.region_0.0_spmd.clone.clone.sunk | while | flops 378539328 | bytes 17040384 | solution.py:68
  79.0 3.5 %fusion.178 = f32[32,128,128]{2,1,0:T(8,128)} fusion(bf16[32,128,128]{2,0,1:T(8,128)(2,1)S(1)} %fusion.177, bf16[96,128,128]{2,1,0:T(8,128)(2,1)} %get-tuple-element.1205, s32[]{:T(128)S(6)} %select_n.52), kind=kOutput, calls=%fused_computation.13.clone.1 | convolution fusion | flops 134217728 | bytes 4194308 | tf_op jit(solution)/shard_map/while/body/eval_jaxpr/mgj,gij->mgi/dot_general | solution.py:53
  97.3 4.1 %bitcast_add_fusion.8 = f32[128,32,128]{2,1,0:T(8,128)} fusion(f32[128,32,128]{2,1,0:T(8,128)} %get-tuple-element.1193, f32[32,128,128]{1,0,2:T(8,128)S(1)} %copy.49, pred[]{:T(512)S(6)} %compare.12, s32[32]{0:T(128)S(1)} %dynamic_slice.142, pred[32]{0:T(512)(128)(4,1)S(1)} %fusion.179), kind=kOutput, calls=%fused_computation.8.clone.1 | convolution fusion | flops 202377216 | bytes 6291617 | tf_op jit(solution)/shard_map/while/body/eval_jaxpr/gp,mgj->mpj/dot_general | solution.py:57
  102.7 3.5 %fusion.178 = f32[32,128,128]{2,1,0:T(8,128)} fusion(bf16[32,128,128]{2,0,1:T(8,128)(2,1)S(1)} %fusion.177, bf16[96,128,128]{2,1,0:T(8,128)(2,1)} %get-tuple-element.1205, s32[]{:T(128)S(6)} %select_n.52), kind=kOutput, calls=%fused_computation.13.clone.1 | convolution fusion | flops 134217728 | bytes 4194308 | tf_op jit(solution)/shard_map/while/body/eval_jaxpr/mgj,gij->mgi/dot_general | solution.py:53
  110.0 4.1 %bitcast_add_fusion.8 = f32[128,32,128]{2,1,0:T(8,128)} fusion(f32[128,32,128]{2,1,0:T(8,128)} %get-tuple-element.1193, f32[32,128,128]{1,0,2:T(8,128)S(1)} %copy.49, pred[]{:T(512)S(6)} %compare.12, s32[32]{0:T(128)S(1)} %dynamic_slice.142, pred[32]{0:T(512)(128)(4,1)S(1)} %fusion.179), kind=kOutput, calls=%fused_computation.8.clone.1 | convolution fusion | flops 202377216 | bytes 6291617 | tf_op jit(solution)/shard_map/while/body/eval_jaxpr/gp,mgj->mpj/dot_general | solution.py:57
  120.3 7.4 %collective-permute-start.3 = (bf16[128,512]{1,0:T(8,128)(2,1)S(1)}, bf16[128,512]{1,0:T(8,128)(2,1)S(1)}, u32[]{:S(2)}, u32[]{:S(2)}) collective-permute-start(bf16[128,512]{1,0:T(8,128)(2,1)S(1)} %get-tuple-element.1005), channel_id=1, source_target_pairs={{0,8},{8,16},{16,24},{24,32},{32,40},{40,48},{48,56},{56,64},{64,7... | collective-permute-start | bytes 393224 | tf_op jit(solution)/shard_map/ppermute | solution.py:18
  131.0 35.3 %while.67 = (s32[]{:T(128)}, f32[128,40,128]{2,1,0:T(8,128)}, bf16[96,128,128]{2,1,0:T(8,128)(2,1)}, s32[96]{0:T(128)}, bf16[128,32,128]{2,1,0:T(8,128)(2,1)S(1)...) while((s32[]{:T(128)}, f32[128,40,128]{2,1,0:T(8,128)}, ...), condition=%wide.region_7.0_spmd.clone.clone, body=%wide.region_6.0_spmd.clone.clone.sunk | while | flops 420744768 | bytes 17826816 | solution.py:68
  137.8 4.5 %bitcast_add_fusion.11 = f32[128,40,128]{2,1,0:T(8,128)} fusion(f32[128,40,128]{2,1,0:T(8,128)} %get-tuple-element.1292, f32[32,128,128]{1,0,2:T(8,128)} %copy.55, pred[]{:T(512)S(6)} %compare.15, s32[32]{0:T(128)S(1)} %dynamic_slice.151, pred[32]{0:T(512)(128)(4,1)S(1)} %fusion.206), kind=kOutput, calls=%fused_computation.65.clone.1 | convolution fusion | flops 252971520 | bytes 7340193 | tf_op jit(solution)/shard_map/while/body/eval_jaxpr/gp,mgj->mpj/dot_general | solution.py:57
  149.1 5.3 %bitcast_add_fusion.11 = f32[128,40,128]{2,1,0:T(8,128)} fusion(f32[128,40,128]{2,1,0:T(8,128)} %get-tuple-element.1292, f32[32,128,128]{1,0,2:T(8,128)} %copy.55, pred[]{:T(512)S(6)} %compare.15, s32[32]{0:T(128)S(1)} %dynamic_slice.151, pred[32]{0:T(512)(128)(4,1)S(1)} %fusion.206), kind=kOutput, calls=%fused_computation.65.clone.1 | convolution fusion | flops 252971520 | bytes 7340193 | tf_op jit(solution)/shard_map/while/body/eval_jaxpr/gp,mgj->mpj/dot_general | solution.py:57
  161.1 5.3 %bitcast_add_fusion.11 = f32[128,40,128]{2,1,0:T(8,128)} fusion(f32[128,40,128]{2,1,0:T(8,128)} %get-tuple-element.1292, f32[32,128,128]{1,0,2:T(8,128)} %copy.55, pred[]{:T(512)S(6)} %compare.15, s32[32]{0:T(128)S(1)} %dynamic_slice.151, pred[32]{0:T(512)(128)(4,1)S(1)} %fusion.206), kind=kOutput, calls=%fused_computation.65.clone.1 | convolution fusion | flops 252971520 | bytes 7340193 | tf_op jit(solution)/shard_map/while/body/eval_jaxpr/gp,mgj->mpj/dot_general | solution.py:57
  173.2 4.0 %collective-permute-start.8 = (bf16[128,4,128]{2,1,0:T(4,128)(2,1)}, bf16[128,4,128]{2,1,0:T(4,128)(2,1)}, u32[]{:S(2)}, u32[]{:S(2)}) collective-permute-start(bf16[128,4,128]{2,1,0:T(4,128)(2,1)} %get-tuple-element.1002), channel_id=1, source_target_pairs={{8,0},{16,8},{24,16},{32,24},{40,32},{48,40},{56,48},{64,56},{72,6... | collective-permute-start | bytes 393224 | tf_op jit(solution)/shard_map/ppermute | solution.py:30
  177.7 36.4 %while.65 = (s32[]{:T(128)}, f32[128,32,128]{2,1,0:T(8,128)}, bf16[96,128,128]{2,1,0:T(8,128)(2,1)}, s32[96]{0:T(128)}, bf16[128,40,128]{2,1,0:T(8,128)(2,1)S(1)...) while((s32[]{:T(128)}, f32[128,32,128]{2,1,0:T(8,128)}, ...), condition=%wide.region_3.0_spmd.clone.clone, body=%wide.region_2.0_spmd.clone.clone.sunk | while | flops 378539328 | bytes 17040384 | solution.py:68
  178.9 3.5 %fusion.187 = f32[32,128,128]{2,1,0:T(8,128)} fusion(bf16[32,128,128]{2,0,1:T(8,128)(2,1)S(1)} %fusion.186, bf16[96,128,128]{2,1,0:T(8,128)(2,1)} %get-tuple-element.1238, s32[]{:T(128)S(6)} %select_n.53), kind=kOutput, calls=%fused_computation.32.clone.1 | convolution fusion | flops 134217728 | bytes 4194308 | tf_op jit(solution)/shard_map/while/body/eval_jaxpr/mgj,gij->mgi/dot_general | solution.py:53
  190.0 3.5 %fusion.187 = f32[32,128,128]{2,1,0:T(8,128)} fusion(bf16[32,128,128]{2,0,1:T(8,128)(2,1)S(1)} %fusion.186, bf16[96,128,128]{2,1,0:T(8,128)(2,1)} %get-tuple-element.1238, s32[]{:T(128)S(6)} %select_n.53), kind=kOutput, calls=%fused_computation.32.clone.1 | convolution fusion | flops 134217728 | bytes 4194308 | tf_op jit(solution)/shard_map/while/body/eval_jaxpr/mgj,gij->mgi/dot_general | solution.py:53
  197.3 4.1 %bitcast_add_fusion.9 = f32[128,32,128]{2,1,0:T(8,128)} fusion(f32[128,32,128]{2,1,0:T(8,128)} %get-tuple-element.1226, f32[32,128,128]{1,0,2:T(8,128)S(1)} %copy.51, pred[]{:T(512)S(6)} %compare.13, s32[32]{0:T(128)S(1)} %dynamic_slice.145, pred[32]{0:T(512)(128)(4,1)S(1)} %fusion.188), kind=kOutput, calls=%fused_computation.27.clone.1 | convolution fusion | flops 202377216 | bytes 6291617 | tf_op jit(solution)/shard_map/while/body/eval_jaxpr/gp,mgj->mpj/dot_general | solution.py:57
  202.6 3.5 %fusion.187 = f32[32,128,128]{2,1,0:T(8,128)} fusion(bf16[32,128,128]{2,0,1:T(8,128)(2,1)S(1)} %fusion.186, bf16[96,128,128]{2,1,0:T(8,128)(2,1)} %get-tuple-element.1238, s32[]{:T(128)S(6)} %select_n.53), kind=kOutput, calls=%fused_computation.32.clone.1 | convolution fusion | flops 134217728 | bytes 4194308 | tf_op jit(solution)/shard_map/while/body/eval_jaxpr/mgj,gij->mgi/dot_general | solution.py:53
  209.9 4.1 %bitcast_add_fusion.9 = f32[128,32,128]{2,1,0:T(8,128)} fusion(f32[128,32,128]{2,1,0:T(8,128)} %get-tuple-element.1226, f32[32,128,128]{1,0,2:T(8,128)S(1)} %copy.51, pred[]{:T(512)S(6)} %compare.13, s32[32]{0:T(128)S(1)} %dynamic_slice.145, pred[32]{0:T(512)(128)(4,1)S(1)} %fusion.188), kind=kOutput, calls=%fused_computation.27.clone.1 | convolution fusion | flops 202377216 | bytes 6291617 | tf_op jit(solution)/shard_map/while/body/eval_jaxpr/gp,mgj->mpj/dot_general | solution.py:57
  (153 shorter events, 126.9 us)
Async XLA Ops:
  0.0 16.3 %collective-permute-start = (bf16[4,32,4096]{2,1,0:T(8,128)(2,1)}, bf16[4,32,4096]{2,1,0:T(8,128)(2,1)S(1)}, u32[]{:S(2)}, u32[]{:S(2)}) collective-permute-start(bf16[4,32,4096]{2,1,0:T(8,128)(2,1)} %param.17), channel_id=1, source_target_pairs={{0,1},{1,2},{2,3},{3,4},{4,5},{5,6},{6,7},{8,9},{9,10},{10,11},{11... | collective-permute-start | bytes 3145736 | tf_op jit(solution)/shard_map/ppermute | solution.py:30
  2.0 14.4 %copy-start.14 = (bf16[2,64,32]{1,2,0:T(8,128)(2,1)S(1)}, bf16[2,64,32]{1,2,0:T(8,128)(2,1)}, u32[]{:S(2)}) copy-start(bf16[2,64,32]{1,2,0:T(8,128)(2,1)} %param.18) | copy-start | bytes 24580
  2.0 14.4 %copy-start.15 = (f32[64]{0:T(128)S(1)}, f32[64]{0:T(128)}, u32[]{:S(2)}) copy-start(f32[64]{0:T(128)} %param.19) | copy-start | bytes 772
  55.0 4.6 %copy-start.1 = (bf16[4,32,4096]{2,1,0:T(8,128)(2,1)S(1)}, bf16[4,32,4096]{2,1,0:T(8,128)(2,1)}, u32[]{:S(2)}) copy-start(bf16[4,32,4096]{2,1,0:T(8,128)(2,1)} %copy-done) | copy-start | bytes 3145732
  57.1 18.4 %copy-start.7 = (bf16[4,32,4096]{2,1,0:T(8,128)(2,1)S(1)}, bf16[4,32,4096]{2,1,0:T(8,128)(2,1)}, u32[]{:S(2)}) copy-start(bf16[4,32,4096]{2,1,0:T(8,128)(2,1)} %param.17) | copy-start | bytes 3145732
  57.1 18.4 %copy-start.13 = (bf16[32,160]{1,0:T(8,128)(2,1)S(1)}, bf16[32,160]{1,0:T(8,128)(2,1)}, u32[]{:S(2)}) copy-start(bf16[32,160]{1,0:T(8,128)(2,1)} %param.20) | copy-start | bytes 30724
  57.1 18.4 %copy-start.16 = (f32[32]{0:T(128)S(1)}, f32[32]{0:T(128)}, u32[]{:S(2)}) copy-start(f32[32]{0:T(128)} %param.21) | copy-start | bytes 388
  59.6 17.7 %collective-permute-start.2 = (bf16[128,512]{1,0:T(8,128)(2,1)S(1)}, bf16[128,512]{1,0:T(8,128)(2,1)S(1)}, u32[]{:S(2)}, u32[]{:S(2)}) collective-permute-start(bf16[128,512]{1,0:T(8,128)(2,1)S(1)} %get-tuple-element.1008), channel_id=1, source_target_pairs={{8,0},{16,8},{24,16},{32,24},{40,32},{48,40},{56,48},{64,56},{72,6... | collective-permute-start | bytes 393224 | tf_op jit(solution)/shard_map/ppermute | solution.py:20
  62.3 15.0 %collective-permute-start.1 = (bf16[128,512]{1,0:T(8,128)(2,1)S(1)}, bf16[128,512]{1,0:T(8,128)(2,1)S(1)}, u32[]{:S(2)}, u32[]{:S(2)}) collective-permute-start(bf16[128,512]{1,0:T(8,128)(2,1)S(1)} %get-tuple-element.1007), channel_id=1, source_target_pairs={{0,8},{8,16},{16,24},{24,32},{32,40},{40,48},{48,56},{56,64},{64,7... | collective-permute-start | bytes 393224 | tf_op jit(solution)/shard_map/ppermute | solution.py:18
  69.6 58.1 %collective-permute-start.5 = (bf16[128,4,128]{2,1,0:T(4,128)(2,1)}, bf16[128,4,128]{2,1,0:T(4,128)(2,1)}, u32[]{:S(2)}, u32[]{:S(2)}) collective-permute-start(bf16[128,4,128]{2,1,0:T(4,128)(2,1)} %get-tuple-element.1003), channel_id=1, source_target_pairs={{0,8},{8,16},{16,24},{24,32},{32,40},{40,48},{48,56},{56,64},{64,7... | collective-permute-start | bytes 393224 | tf_op jit(solution)/shard_map/ppermute | solution.py:30
  71.5 56.2 %collective-permute-start.6 = (bf16[128,4,128]{2,1,0:T(4,128)(2,1)}, bf16[128,4,128]{2,1,0:T(4,128)(2,1)}, u32[]{:S(2)}, u32[]{:S(2)}) collective-permute-start(bf16[128,4,128]{2,1,0:T(4,128)(2,1)} %get-tuple-element.1004), channel_id=1, source_target_pairs={{8,0},{16,8},{24,16},{32,24},{40,32},{48,40},{56,48},{64,56},{72,6... | collective-permute-start | bytes 393224 | tf_op jit(solution)/shard_map/ppermute | solution.py:30
  117.2 12.0 %copy-start.12 = (bf16[128,24,128]{2,1,0:T(8,128)(2,1)S(1)}, bf16[128,24,128]{2,1,0:T(8,128)(2,1)}, u32[]{:S(2)}) copy-start(bf16[128,24,128]{2,1,0:T(8,128)(2,1)} %slice.95) | copy-start | bytes 2359300
  117.6 11.5 %copy-start.4 = (bf16[16,8,32,128]{3,1,2,0:T(8,128)(2,1)}, bf16[16,8,32,128]{3,1,2,0:T(8,128)(2,1)S(1)}, u32[]{:S(2)}) copy-start(bf16[16,8,32,128]{3,1,2,0:T(8,128)(2,1)S(1)} %copy.39) | copy-start | bytes 3145732
  118.4 58.9 %collective-permute-start.4 = (bf16[128,512]{1,0:T(8,128)(2,1)}, bf16[128,512]{1,0:T(8,128)(2,1)S(1)}, u32[]{:S(2)}, u32[]{:S(2)}) collective-permute-start(bf16[128,512]{1,0:T(8,128)(2,1)} %get-tuple-element.1006), channel_id=1, source_target_pairs={{8,0},{16,8},{24,16},{32,24},{40,32},{48,40},{56,48},{64,56},{72,6... | collective-permute-start | bytes 393224 | tf_op jit(solution)/shard_map/ppermute | solution.py:20
  120.3 57.0 %collective-permute-start.3 = (bf16[128,512]{1,0:T(8,128)(2,1)S(1)}, bf16[128,512]{1,0:T(8,128)(2,1)S(1)}, u32[]{:S(2)}, u32[]{:S(2)}) collective-permute-start(bf16[128,512]{1,0:T(8,128)(2,1)S(1)} %get-tuple-element.1005), channel_id=1, source_target_pairs={{0,8},{8,16},{16,24},{24,32},{32,40},{40,48},{48,56},{56,64},{64,7... | collective-permute-start | bytes 393224 | tf_op jit(solution)/shard_map/ppermute | solution.py:18
  166.4 5.0 %copy-start.3 = (f32[4,32,4096]{2,1,0:T(8,128)S(1)}, f32[4,32,4096]{2,1,0:T(8,128)}, u32[]{:S(2)}) copy-start(f32[4,32,4096]{2,1,0:T(8,128)} %fusion.98) | copy-start | bytes 6291460
  166.4 5.0 %copy-start.9 = (bf16[4,32,4096]{2,1,0:T(8,128)(2,1)S(1)}, bf16[4,32,4096]{2,1,0:T(8,128)(2,1)}, u32[]{:S(2)}) copy-start(bf16[4,32,4096]{2,1,0:T(8,128)(2,1)} %convert_element_type.118) | copy-start | bytes 3145732
  168.5 4.7 %copy-start.6 = (bf16[128,40,128]{2,1,0:T(8,128)(2,1)}, bf16[128,40,128]{2,1,0:T(8,128)(2,1)S(1)}, u32[]{:S(2)}) copy-start(bf16[128,40,128]{2,1,0:T(8,128)(2,1)S(1)} %convert.17) | copy-start | bytes 3932164
  169.4 47.7 %collective-permute-start.7 = (bf16[128,4,128]{2,1,0:T(4,128)(2,1)}, bf16[128,4,128]{2,1,0:T(4,128)(2,1)}, u32[]{:S(2)}, u32[]{:S(2)}) collective-permute-start(bf16[128,4,128]{2,1,0:T(4,128)(2,1)} %get-tuple-element.1001), channel_id=1, source_target_pairs={{0,8},{8,16},{16,24},{24,32},{32,40},{40,48},{48,56},{56,64},{64,7... | collective-permute-start | bytes 393224 | tf_op jit(solution)/shard_map/ppermute | solution.py:30
  173.2 4.1 %copy-start.5 = (bf16[16,8,32,128]{3,1,2,0:T(8,128)(2,1)S(1)}, bf16[16,8,32,128]{3,1,2,0:T(8,128)(2,1)}, u32[]{:S(2)}) copy-start(bf16[16,8,32,128]{3,1,2,0:T(8,128)(2,1)} %copy-done.4) | copy-start | bytes 3145732
  173.2 43.9 %collective-permute-start.8 = (bf16[128,4,128]{2,1,0:T(4,128)(2,1)}, bf16[128,4,128]{2,1,0:T(4,128)(2,1)}, u32[]{:S(2)}, u32[]{:S(2)}) collective-permute-start(bf16[128,4,128]{2,1,0:T(4,128)(2,1)} %get-tuple-element.1002), channel_id=1, source_target_pairs={{8,0},{16,8},{24,16},{32,24},{40,32},{48,40},{56,48},{64,56},{72,6... | collective-permute-start | bytes 393224 | tf_op jit(solution)/shard_map/ppermute | solution.py:30
  215.8 2.7 %slice-start = ((bf16[128,40,128]{2,1,0:T(8,128)(2,1)}), bf16[128,24,128]{2,1,0:T(8,128)(2,1)S(1)}, s32[]{:S(2)}) async-start(bf16[128,40,128]{2,1,0:T(8,128)(2,1)} %copy-done.6), calls=%async_computation | async-start | bytes 1572864 | tf_op jit(solution)/shard_map/slice | solution.py:92
  218.6 4.0 %copy-start.2 = (f32[4,32,4096]{2,1,0:T(8,128)S(1)}, f32[4,32,4096]{2,1,0:T(8,128)}, u32[]{:S(2)}) copy-start(f32[4,32,4096]{2,1,0:T(8,128)} %fusion.97) | copy-start | bytes 6291460
  220.1 2.4 %copy-start.10 = (bf16[4,32,4096]{2,1,0:T(8,128)(2,1)S(1)}, bf16[4,32,4096]{2,1,0:T(8,128)(2,1)}, u32[]{:S(2)}) copy-start(bf16[4,32,4096]{2,1,0:T(8,128)(2,1)} %convert_element_type.121) | copy-start | bytes 3145732
  (3 other events, 3.4 us)
where the time goes:
time: 229 us; the launch traced here: 226 us
  matrix products  101 us (44%)
  local copies, waits for them, and re-layouts  58.9 us (26%)
  starting transfers between devices  32.2 us (14%)
  other arithmetic  21.5 us (9%)
  waiting for transfers between devices  12.3 us (5%)
    dot_general x12, matrix products, add_block(): jnp.einsum('gp,mgj->mpj', placer, products, precision=lax.Precision.HIGHE...  51.8 us
    dot_general x12, matrix products, add_block(): jnp.einsum(equation, panels, block_values, preferred_element_type=jnp.flo...  34 us
    dot_general x12, local copies, waits for them, and re-layouts, add_block(): jnp.einsum(equation, panels, block_values, preferred_element_type=jnp.flo...  26.4 us
    ppermute x2, starting transfers between devices, padded(): lax.ppermute(tail, axis, [(i, (i + 1) % count) for i in range(ends)])  13.9 us
    ppermute x5, starting transfers between devices, shifted(): return lax.ppermute(shard, axis, pairs)  13.7 us
    ppermute x5, waiting for transfers between devices, shifted(): return lax.ppermute(shard, axis, pairs)  12.3 us
    dynamic_slice x12, local copies, waits for them, and re-layouts, add_block(): block_put = lax.dynamic_slice_in_dim(put_index, first_slot, group_size, 0)  8.77 us
    dynamic_slice x12, local copies, waits for them, and re-layouts, add_block(): block_take = lax.dynamic_slice_in_dim(take_index, first_slot, group_size, 0)  8.74 us
  transfers between devices with their start and end apart: 9, of which 1 were waited for; matrix products, arithmetic and copies ran while one was open for 57% of the time, Pallas kernels for 0%

commit v1 on v0

v1 whole, which is shorter than its diff:
```python
import jax
import jax.numpy as jnp
from jax import lax
from jax.experimental import pallas as pl
from jax.experimental.pallas import tpu as pltpu
from jax.sharding import PartitionSpec as P

HB = 4
DAYS = 4
CH = 32
T = 128
ROWS = DAYS * CH
SLOTS = 96
RT = 32
EXTRA = SLOTS - RT
CHUNK = 4
CHUNKS = RT // CHUNK
MESH = pl.DeviceIdType.MESH
F32 = jnp.float32
BF16 = jnp.bfloat16
I32 = jnp.int32


def iota(shape, dim):
    return lax.broadcasted_iota(I32, shape, dim)


def nn(a, b):
    return jnp.dot(a, b, preferred_element_type=F32)


def nt(a, b):
    return lax.dot_general(a, b, (((1,), (1,)), ((), ())), preferred_element_type=F32)


def segments(keys, takes):
    square = (T, T)
    slot_row = iota(square, 0)
    slot_col = iota(square, 1)
    by_col = jnp.broadcast_to(keys, square)
    by_row = by_col.T
    take_row = jnp.broadcast_to(takes, square).T
    earlier_same = ((by_col == by_row) & (slot_col < slot_row)).astype(I32)
    lower = (by_col < by_row).astype(I32)
    rank = jnp.sum(earlier_same + lower, axis=1, keepdims=True)
    keep = (jnp.sum(earlier_same, axis=1, keepdims=True) > 0).astype(I32)
    at = rank == slot_col
    zero = jnp.zeros(square, I32)
    perm = jnp.sum(jnp.where(at, jnp.minimum(slot_row, SLOTS - 1), zero), axis=0, keepdims=True)
    take = jnp.sum(jnp.where(at, take_row, zero), axis=0, keepdims=True)
    kept = jnp.sum(jnp.where(at, jnp.broadcast_to(keep, square), zero), axis=0, keepdims=True)
    upto = jnp.sum((by_row <= slot_col).astype(I32), axis=0, keepdims=True)
    count = jnp.sum((by_row == slot_col).astype(I32), axis=0, keepdims=True)
    last = jnp.where(count > 0, upto, 0)
    return perm, take, kept, last


def kernel(
    signal_ref,
    time_weight_ref,
    time_bias_ref,
    mix_weight_ref,
    mix_bias_ref,
    tiles_hbm,
    rows_ref,
    cols_ref,
    count_ref,
    out_hbm,
    cur,
    lag,
    tiles,
    hidden,
    fwd,
    bwd,
    sums_f,
    sums_b,
    rim_out,
    rim_in,
    rim_out2,
    rim_in2,
    out,
    conv_w,
    mix_w,
    table_v,
    table,
    local_sem,
    x_send,
    x_recv,
    r_send,
    r_recv,
    out_sem,
):
    region = lax.axis_index("region")
    tm = lax.axis_index("tm")
    regions = lax.axis_size("region")
    tms = lax.axis_size("tm")
    above = (lax.rem(region + 1, regions), tm)
    below = (lax.rem(region + regions - 1, regions), tm)
    later = (region, lax.rem(tm + 1, tms))
    earlier = (region, lax.rem(tm + tms - 1, tms))

    barrier = pltpu.get_barrier_semaphore()
    for peer in (above, below, later, earlier):
        pl.semaphore_signal(barrier, inc=1, device_id=peer, device_id_type=MESH)

    load_signal = pltpu.make_async_copy(signal_ref, cur, local_sem.at[0])
    load_signal.start()
    load_tiles = pltpu.make_async_copy(tiles_hbm, tiles, local_sem.at[1])
    load_tiles.start()
    pl.semaphore_wait(barrier, 4)

    def chunk_of(turn):
        return jnp.where(turn == 0, 0, jnp.where(turn == 1, CHUNKS - 1, turn - 1))

    def columns(chunk):
        return pl.ds(pl.multiple_of(chunk * (CHUNK * T), CHUNK * T), CHUNK * T)

    def shift(turn):
        where = columns(chunk_of(turn))
        return pltpu.make_async_remote_copy(
            src_ref=signal_ref.at[:, where],
            dst_ref=lag.at[:, where],
            send_sem=x_send.at[turn],
            recv_sem=x_recv.at[turn],
            device_id=later,
            device_id_type=MESH,
        )

    def start_shift(turn, carry):
        shift(turn).start()
        return carry

    lax.fori_loop(0, CHUNKS, start_shift, 0)

    lane = iota((1, T), 1)
    pad = jnp.zeros((1, T - SLOTS), I32)
    rows = jnp.concatenate([rows_ref[...], pad], axis=1)
    cols = jnp.concatenate([cols_ref[...], pad], axis=1)
    live = (lane >= RT) & (lane < count_ref[0])
    far = jnp.full((1, T), 2 * T, I32)
    perm_f, take_f, keep_f, last_f = segments(jnp.where(live, rows, far), cols)
    perm_b, take_b, keep_b, last_b = segments(jnp.where(live, cols, far), rows)
    table_v[...] = jnp.concatenate(
        [perm_f, take_f, keep_f, last_f, perm_b, take_b, keep_b, last_b], axis=0
    )
    to_scalars = pltpu.make_async_copy(table_v, table, local_sem.at[2])
    to_scalars.start()

    spread = (lax.rem(iota((ROWS, CH), 0), CH) == iota((ROWS, CH), 1)).astype(BF16)
    same_day = iota((ROWS, ROWS), 0) // CH == iota((ROWS, ROWS), 1) // CH
    for part in range(2):
        scale = 1.0 if part == 0 else 0.5
        for tap in range(2):
            block = time_weight_ref[tap, part * CH : (part + 1) * CH, :]
            wide = nt(nn(spread, block).astype(BF16), spread)
            conv_w[part * ROWS : (part + 1) * ROWS, tap * ROWS : (tap + 1) * ROWS] = jnp.where(
                same_day, wide * scale, 0.0
            ).astype(BF16)
    tall_mix = nn(spread, mix_weight_ref[...]).astype(BF16)
    for branch in range(5):
        pick = (
            iota((5 * CH, ROWS), 0) == branch * CH + lax.rem(iota((5 * CH, ROWS), 1), CH)
        ).astype(BF16)
        mix_w[:, branch * ROWS : (branch + 1) * ROWS] = jnp.where(
            same_day, nn(tall_mix, pick), 0.0
        ).astype(BF16)
    channel = lax.rem(iota((ROWS, 1), 0), CH)

    def column_of(values, first):
        width = values.shape[1]
        hit = iota((ROWS, width), 1) == channel + first
        return jnp.sum(jnp.where(hit, jnp.broadcast_to(values, (ROWS, width)), 0.0), 1, keepdims=True)

    time_bias = time_bias_ref[...].reshape(1, 2 * CH)
    bias_filter = column_of(time_bias, 0)
    bias_gate = column_of(time_bias, CH) * 0.5
    bias_mix = column_of(mix_bias_ref[...].reshape(1, CH), 0)

    sums_f[0] = jnp.zeros((T, T), F32)
    sums_b[0] = jnp.zeros((T, T), F32)

    def to_region(src, dst, index, peer):
        return pltpu.make_async_remote_copy(
            src_ref=src,
            dst_ref=dst,
            send_sem=r_send.at[index],
            recv_sem=r_recv.at[index],
            device_id=peer,
            device_id_type=MESH,
        )

    halo_low = to_region(hidden.at[pl.ds(HB, HB)], hidden.at[pl.ds(HB + RT, HB)], 0, below)
    halo_high = to_region(hidden.at[pl.ds(RT, HB)], hidden.at[pl.ds(0, HB)], 1, above)
    rim_low = to_region(rim_out.at[pl.ds(0, HB)], rim_in.at[pl.ds(HB, HB)], 2, below)
    rim_high = to_region(rim_out.at[pl.ds(HB, HB)], rim_in.at[pl.ds(0, HB)], 3, above)
    fwd_low = to_region(fwd.at[pl.ds(HB, HB)], fwd.at[pl.ds(HB + RT, HB)], 4, below)
    fwd_high = to_region(fwd.at[pl.ds(RT, HB)], fwd.at[pl.ds(0, HB)], 5, above)
    rim2_low = to_region(rim_out2.at[pl.ds(0, HB)], rim_in2.at[pl.ds(HB, HB)], 6, below)
    rim2_high = to_region(rim_out2.at[pl.ds(HB, HB)], rim_in2.at[pl.ds(0, HB)], 7, above)

    load_signal.wait()
    first_block = jnp.where(tm == 0, 0.0, 1.0).astype(BF16)

    def gate(turn, carry):
        chunk = chunk_of(turn)
        where = columns(chunk)
        shift(turn).wait_recv()
        pre = nn(conv_w[:, :ROWS], lag[:, where] * first_block) + nn(conv_w[:, ROWS:], cur[:, where])
        value = jnp.tanh(pre[:ROWS] + bias_filter) * (0.5 + 0.5 * jnp.tanh(pre[ROWS:] + bias_gate))
        value = value.astype(BF16)
        for tile in range(CHUNK):
            hidden[HB + chunk * CHUNK + tile] = value[:, tile * T : (tile + 1) * T]
        return carry

    gate(0, 0)
    halo_low.start()
    gate(1, 0)
    halo_high.start()
    lax.fori_loop(2, CHUNKS, gate, 0)
    to_scalars.wait()
    load_tiles.wait()

    def extras_f(source):
        def add(place, running):
            product = nt(source[table[1, place]], tiles[table[0, place]])
            running = jnp.where(table[2, place] > 0, running, 0.0) + product
            sums_f[place + 1] = running
            return running

        lax.fori_loop(0, EXTRA, add, jnp.zeros((T, T), F32), unroll=4)

    def extras_b(source, base):
        def add(place, running):
            product = nn(source[table[5, place] + base], tiles[table[4, place]])
            running = jnp.where(table[6, place] > 0, running, 0.0) + product
            sums_b[place + 1] = running
            return running

        lax.fori_loop(0, EXTRA, add, jnp.zeros((T, T), F32), unroll=4)

    def rims(target):
        def fill(tile, carry):
            target[tile] = sums_b[table[7, tile]].astype(BF16)
            target[HB + tile] = sums_b[table[7, HB + RT + tile]].astype(BF16)
            return carry

        lax.fori_loop(0, HB, fill, 0)

    def forward(source, tile):
        return nt(source[HB + tile], tiles[tile]) + sums_f[table[3, tile]]

    def backward(source, base, tile):
        return nn(source[base + tile], tiles[tile]) + sums_b[table[7, HB + tile]]

    halo_low.wait()
    halo_high.wait()
    extras_b(hidden, HB)
    rims(rim_out)
    rim_low.start()
    rim_high.start()
    extras_f(hidden)

    def fwd_tile(tile, carry):
        fwd[HB + tile] = forward(hidden, tile).astype(BF16)
        return carry

    lax.fori_loop(0, HB, fwd_tile, 0)
    fwd_low.start()
    lax.fori_loop(RT - HB, RT, fwd_tile, 0)
    fwd_high.start()
    lax.fori_loop(HB, RT - HB, fwd_tile, 0, unroll=4)

    def bwd_tile(tile, carry):
        bwd[tile] = backward(hidden, HB, tile).astype(BF16)
        return carry

    lax.fori_loop(HB, RT - HB, bwd_tile, 0, unroll=4)
    rim_low.wait()
    rim_high.wait()

    def bwd_rim(tile, carry):
        low, high = tile, RT - HB + tile
        bwd[low] = (backward(hidden, HB, low) + rim_in[tile].astype(F32)).astype(BF16)
        bwd[high] = (backward(hidden, HB, high) + rim_in[HB + tile].astype(F32)).astype(BF16)
        return carry

    lax.fori_loop(0, HB, bwd_rim, 0)

    extras_b(bwd, 0)
    rims(rim_out2)
    rim2_low.start()
    rim2_high.start()
    fwd_low.wait()
    fwd_high.wait()
    extras_f(fwd)

    def mixed(tile, rim):
        two = backward(bwd, 0, tile)
        if rim is not None:
            two = two + rim.astype(F32)
        blocks = jnp.concatenate(
            [
                hidden[HB + tile],
                fwd[HB + tile],
                forward(fwd, tile).astype(BF16),
                bwd[tile],
                two.astype(BF16),
            ],
            axis=0,
        )
        where = pl.ds(pl.multiple_of(tile * T, T), T)
        total = nn(mix_w[...], blocks) + cur[:, where].astype(F32) + bias_mix
        out[:, where] = total.astype(BF16)

    def mix_inner(tile, carry):
        mixed(tile, None)
        return carry

    def store(first, count, index):
        where = pl.ds(first * T, count * T)
        return pltpu.make_async_copy(out.at[:, where], out_hbm.at[:, where], out_sem.at[index])

    lax.fori_loop(HB, RT - HB, mix_inner, 0, unroll=2)
    inner_store = store(HB, RT - 2 * HB, 0)
    inner_store.start()
    rim2_low.wait()
    rim2_high.wait()

    def mix_rim(tile, carry):
        mixed(tile, rim_in2[tile])
        mixed(RT - HB + tile, rim_in2[HB + tile])
        return carry

    lax.fori_loop(0, HB, mix_rim, 0)
    low_store = store(0, HB, 1)
    high_store = store(RT - HB, HB, 2)
    low_store.start()
    high_store.start()

    def end_shift(turn, carry):
        shift(turn).wait_send()
        return carry

    lax.fori_loop(0, CHUNKS, end_shift, 0)
    inner_store.wait()
    low_store.wait()
    high_store.wait()


def body(
    signal,
    time_weight,
    time_bias,
    mix_weight,
    mix_bias,
    tile_values,
    tile_rows,
    tile_cols,
    tile_count,
):
    width = signal.shape[2]
    anywhere = pl.BlockSpec(memory_space=pl.ANY)
    vmem = pl.BlockSpec(memory_space=pltpu.VMEM)
    smem = pl.BlockSpec(memory_space=pltpu.SMEM)
    panel = pltpu.VMEM((ROWS, width), BF16)
    result = pl.pallas_call(
        kernel,
        out_shape=jax.ShapeDtypeStruct((ROWS, width), BF16),
        in_specs=[anywhere, vmem, vmem, vmem, vmem, anywhere, vmem, vmem, smem],
        out_specs=anywhere,
        scratch_shapes=[
            panel,
            panel,
            pltpu.VMEM((SLOTS, T, T), BF16),
            pltpu.VMEM((RT + 2 * HB, ROWS, T), BF16),
            pltpu.VMEM((RT + 2 * HB, ROWS, T), BF16),
            pltpu.VMEM((RT, ROWS, T), BF16),
            pltpu.VMEM((EXTRA + 1, ROWS, T), F32),
            pltpu.VMEM((EXTRA + 1, ROWS, T), F32),
            pltpu.VMEM((2 * HB, ROWS, T), BF16),
            pltpu.VMEM((2 * HB, ROWS, T), BF16),
            pltpu.VMEM((2 * HB, ROWS, T), BF16),
            pltpu.VMEM((2 * HB, ROWS, T), BF16),
            panel,
            pltpu.VMEM((2 * ROWS, 2 * ROWS), BF16),
            pltpu.VMEM((ROWS, 5 * ROWS), BF16),
            pltpu.VMEM((8, T), I32),
            pltpu.SMEM((8, T), I32),
            pltpu.SemaphoreType.DMA((3,)),
            pltpu.SemaphoreType.DMA((CHUNKS,)),
            pltpu.SemaphoreType.DMA((CHUNKS,)),
            pltpu.SemaphoreType.DMA((8,)),
            pltpu.SemaphoreType.DMA((8,)),
            pltpu.SemaphoreType.DMA((3,)),
        ],
        compiler_params=pltpu.CompilerParams(
            collective_id=0, has_side_effects=True, vmem_limit_bytes=56 * 2**20
        ),
    )(
        signal.reshape(ROWS, width),
        time_weight,
        time_bias,
        mix_weight,
        mix_bias,
        tile_values[0],
        tile_rows,
        tile_cols,
        tile_count,
    )
    return result.reshape(signal.shape)


def solution(mesh):
    placed = (
        P("tm", None, "region"),
        P(),
        P(),
        P(),
        P(),
        P("region", None, None, None),
        P("region", None),
        P("region", None),
        P("region"),
    )
    return jax.shard_map(
        body, mesh=mesh, in_specs=placed, out_specs=P("tm", None, "region"), check_vma=False
    )
```

time: 229 us -> 52.9 us (0.23)
  the two profiles are of different devices: /device:TPU:126 before, /device:TPU:0 now
where the time goes in v1:
time: 52.9 us; the launch traced here: 52.7 us
  Pallas kernels  48.3 us (91%)
  local copies, waits for them, and re-layouts  3.71 us (7%)
  between operations  0.66 us (1%)
    pallas_call x1, Pallas kernels, body(): pl.pallas_call(kernel, out_shape=jax.ShapeDtypeStruct((ROWS, width), BF16...  48.3 us
    unnamed x2, local copies, waits for them, and re-layouts  3.71 us

profile of v1, /device:TPU:0, one launch (start us, length us, event | category | flops | bytes accessed | tf_op | source)
XLA Modules:
  0.0 52.7 jit_solution(1971764494463422887)
XLA Ops:
  0.7 1.4 %copy.10.time_weight_ref = bf16[2,64,32]{2,1,0:T(8,128)(2,1)} copy(bf16[2,64,32]{1,2,0:T(8,128)(2,1)} %param.10) | data formatting | bytes 16384 | tf_op args[1]
  2.1 48.3 %shard_map.91 = bf16[128,4096]{1,0:T(8,128)(2,1)} custom-call(bf16[128,4096]{1,0:T(8,128)(2,1)} %bitcast.5, bf16[2,64,32]{2,1,0:T(8,128)(2,1)} %copy.10.time_weight_ref, f32[64]{0:T(128)} %time_bias_ref.1, bf16[32,160]{1,0:T(8,128)(2,1)} %mix_weight_ref.1, f32[32]{0:T(128)} %mix_bias_ref.1, bf16[96,128,128]{2,1,0:T(8,128)(2,1)} %bitcast.4, ...), custom_call_target="tpu_custom_call" | custom-call | tf_op jit(solution)/shard_map/pallas_call | solution.py:366
  50.4 2.3 %copy.13 = bf16[4,32,4096]{2,1,0:T(8,128)(2,1)} copy(bf16[4,32,4096]{2,1,0:T(8,128)(2,1)} %bitcast.3) | data formatting | bytes 2097152

commit v2 on v1

v2 whole, which is shorter than its diff:
```python
import jax
import jax.numpy as jnp
from jax import lax
from jax.experimental import pallas as pl
from jax.experimental.pallas import tpu as pltpu
from jax.sharding import PartitionSpec as P

HB = 4
DAYS = 4
CH = 32
T = 128
GROUPS = 1
ROWS = DAYS * CH // GROUPS
SLOTS = 96
RT = 32
EXTRA = SLOTS - RT
CHUNK = 8 if GROUPS == 2 else 4
PAIR = 2
UNROLL = 64
INNER = 12
MIXED = 4
CHUNKS = RT // CHUNK
MESH = pl.DeviceIdType.MESH
F32 = jnp.float32
BF16 = jnp.bfloat16
I32 = jnp.int32


def iota(shape, dim):
    return lax.broadcasted_iota(I32, shape, dim)


def nn(a, b):
    return jnp.dot(a, b, preferred_element_type=F32)


def segments(keys, takes):
    square = (T, T)
    slot_row = iota(square, 0)
    slot_col = iota(square, 1)
    by_col = jnp.broadcast_to(keys, square)
    by_row = by_col.T
    take_row = jnp.broadcast_to(takes, square).T
    earlier_same = ((by_col == by_row) & (slot_col < slot_row)).astype(I32)
    lower = (by_col < by_row).astype(I32)
    rank = jnp.sum(earlier_same + lower, axis=1, keepdims=True)
    keep = (jnp.sum(earlier_same, axis=1, keepdims=True) > 0).astype(I32)
    at = rank == slot_col
    zero = jnp.zeros(square, I32)
    perm = jnp.sum(jnp.where(at, jnp.minimum(slot_row, SLOTS - 1), zero), axis=0, keepdims=True)
    take = jnp.sum(jnp.where(at, take_row, zero), axis=0, keepdims=True)
    kept = jnp.sum(jnp.where(at, jnp.broadcast_to(keep, square), zero), axis=0, keepdims=True)
    upto = jnp.sum((by_row <= slot_col).astype(I32), axis=0, keepdims=True)
    count = jnp.sum((by_row == slot_col).astype(I32), axis=0, keepdims=True)
    last = jnp.where(count > 0, upto, 0)
    return perm, take, kept, last


def kernel(
    signal_ref,
    time_weight_hbm,
    time_bias_hbm,
    mix_weight_hbm,
    mix_bias_hbm,
    tiles_hbm,
    rows_hbm,
    cols_hbm,
    count_hbm,
    out_ref,
    cur,
    lag,
    tiles,
    tiles_t,
    hidden,
    fwd,
    bwd,
    sums_f,
    sums_b,
    rim_out,
    rim_in,
    rim_out2,
    rim_in2,
    out,
    conv_w,
    mix_w,
    time_weight_ref,
    time_bias_ref,
    mix_weight_ref,
    mix_bias_ref,
    rows_ref,
    cols_ref,
    count_ref,
    table_v,
    table,
    local_sem,
    x_send,
    x_recv,
    r_send,
    r_recv,
    out_sem,
):
    region = lax.axis_index("region")
    tm = lax.axis_index("tm")
    regions = lax.axis_size("region")
    tms = lax.axis_size("tm")
    above = (lax.rem(region + 1, regions), tm)
    below = (lax.rem(region + regions - 1, regions), tm)
    later = (region, lax.rem(tm + 1, tms))
    earlier = (region, lax.rem(tm + tms - 1, tms))

    barrier = pltpu.get_barrier_semaphore()
    for peer in (later, earlier, above, below):
        pl.semaphore_signal(barrier, inc=1, device_id=peer, device_id_type=MESH)

    loads = [
        pltpu.make_async_copy(src, dst, local_sem.at[index])
        for index, (src, dst) in enumerate(
            [
                (count_hbm, count_ref),
                (rows_hbm, rows_ref),
                (cols_hbm, cols_ref),
                (time_weight_hbm, time_weight_ref),
                (time_bias_hbm, time_bias_ref),
                (mix_weight_hbm, mix_weight_ref),
                (mix_bias_hbm, mix_bias_ref),
                (signal_ref, cur),
                (tiles_hbm, tiles),
            ]
        )
    ]
    for load in loads:
        load.start()
    pl.semaphore_wait(barrier, 4)

    def columns(chunk):
        return pl.ds(chunk * (CHUNK * T), CHUNK * T)

    def shift(group, chunk):
        where = (pl.ds(group * ROWS, ROWS), columns(chunk))
        index = group * CHUNKS + chunk
        return pltpu.make_async_remote_copy(
            src_ref=signal_ref.at[where],
            dst_ref=lag.at[where],
            send_sem=x_send.at[index],
            recv_sem=x_recv.at[index],
            device_id=later,
            device_id_type=MESH,
        )

    order = [0, CHUNKS - 1] + list(range(1, CHUNKS - 1))
    for group in range(GROUPS):
        for chunk in order:
            shift(group, chunk).start()
    for load in loads[:7]:
        load.wait()

    spread = (lax.rem(iota((ROWS, CH), 0), CH) == iota((ROWS, CH), 1)).astype(BF16)
    same_day = iota((ROWS, ROWS), 0) // CH == iota((ROWS, ROWS), 1) // CH
    has_earlier = jnp.where(tm == 0, 0.0, 1.0)
    for part in range(2):
        tall = [nn(spread, time_weight_ref[tap]).astype(BF16) for tap in range(2)]
        pick = (
            iota((2 * CH, ROWS), 0) == part * CH + lax.rem(iota((2 * CH, ROWS), 1), CH)
        ).astype(BF16)
        for tap in range(2):
            wide = nn(tall[tap], pick).T * (1.0 if part == 0 else 0.5)
            if tap == 0:
                wide = wide * has_earlier
            conv_w[part * ROWS : (part + 1) * ROWS, tap * ROWS : (tap + 1) * ROWS] = jnp.where(
                same_day, wide, 0.0
            ).astype(BF16)
    tall_mix = nn(spread, mix_weight_ref[...]).astype(BF16)
    for branch in range(5):
        pick = (
            iota((5 * CH, ROWS), 0) == branch * CH + lax.rem(iota((5 * CH, ROWS), 1), CH)
        ).astype(BF16)
        mix_w[:, branch * ROWS : (branch + 1) * ROWS] = jnp.where(
            same_day, nn(tall_mix, pick), 0.0
        ).astype(BF16)
    channel = lax.rem(iota((ROWS, 1), 0), CH)

    def column_of(values, first):
        width = values.shape[1]
        hit = iota((ROWS, width), 1) == channel + first
        return jnp.sum(jnp.where(hit, jnp.broadcast_to(values, (ROWS, width)), 0.0), 1, keepdims=True)

    time_bias = time_bias_ref[...].reshape(1, 2 * CH)
    bias_filter = column_of(time_bias, 0)
    bias_gate = column_of(time_bias, CH) * 0.5
    bias_mix = column_of(mix_bias_ref[...].reshape(1, CH), 0)
    loads[7].wait()

    def to_region(src, dst, index, peer):
        return pltpu.make_async_remote_copy(
            src_ref=src,
            dst_ref=dst,
            send_sem=r_send.at[index],
            recv_sem=r_recv.at[index],
            device_id=peer,
            device_id_type=MESH,
        )

    first_tiles, last_tiles = pl.ds(HB, HB), pl.ds(RT, HB)
    from_below, from_above = pl.ds(0, HB), pl.ds(HB + RT, HB)
    rim_first, rim_last = pl.ds(0, HB), pl.ds(HB, HB)
    halo, rim, edge, rim2 = [], [], [], []
    for g in range(GROUPS):
        base = 8 * g
        halo.append(
            (
                to_region(hidden[g].at[first_tiles], hidden[g].at[from_above], base, below),
                to_region(hidden[g].at[last_tiles], hidden[g].at[from_below], base + 1, above),
            )
        )
        rim.append(
            (
                to_region(rim_out[g].at[rim_first], rim_in[g].at[rim_last], base + 2, below),
                to_region(rim_out[g].at[rim_last], rim_in[g].at[rim_first], base + 3, above),
            )
        )
        edge.append(
            (
                to_region(fwd[g].at[first_tiles], fwd[g].at[from_above], base + 4, below),
                to_region(fwd[g].at[last_tiles], fwd[g].at[from_below], base + 5, above),
            )
        )
        rim2.append(
            (
                to_region(rim_out2[g].at[rim_first], rim_in2[g].at[rim_last], base + 6, below),
                to_region(rim_out2[g].at[rim_last], rim_in2[g].at[rim_first], base + 7, above),
            )
        )

    def gate(group, chunk):
        shift(group, chunk).wait_recv()
        rows_here = pl.ds(group * ROWS, ROWS)

        def part(index, carry):
            first = chunk * CHUNK + index * PAIR
            where = pl.ds(pl.multiple_of(first * T, PAIR * T), PAIR * T)
            days = jnp.concatenate([lag[rows_here, where], cur[rows_here, where]], axis=0)
            pre = nn(conv_w[...], days)
            value = jnp.tanh(pre[:ROWS] + bias_filter) * (
                0.5 + 0.5 * jnp.tanh(pre[ROWS:] + bias_gate)
            )
            value = value.astype(BF16)
            for tile in range(PAIR):
                hidden[group][HB + first + tile] = value[:, tile * T : (tile + 1) * T]
            return carry

        lax.fori_loop(0, CHUNK // PAIR, part, 0, unroll=CHUNK // PAIR)

    def outer_gates(group):
        gate(group, 0)
        halo[group][0].start()
        gate(group, CHUNKS - 1)
        halo[group][1].start()

    def inner_gates(group):
        for chunk in range(1, CHUNKS - 1):
            gate(group, chunk)

    def extras(source, base, values, sums, first):
        def add(place, running):
            product = nn(source[table[first + 1, place] + base], values[table[first, place]])
            running = jnp.where(table[first + 2, place] > 0, running, 0.0) + product
            sums[place + 1] = running
            return running

        lax.fori_loop(0, EXTRA, add, jnp.zeros((ROWS, T), F32), unroll=UNROLL)

    def extras_f(g, source):
        extras(source, 0, tiles_t, sums_f[g], 0)

    def extras_b(g, source, base):
        extras(source, base, tiles, sums_b[g], 4)

    def rims(g, target):
        def fill(tile, carry):
            target[tile] = sums_b[g][table[7, tile]].astype(BF16)
            target[HB + tile] = sums_b[g][table[7, HB + RT + tile]].astype(BF16)
            return carry

        lax.fori_loop(0, HB, fill, 0, unroll=HB)

    def forward(g, source, tile):
        return nn(source[HB + tile], tiles_t[tile]) + sums_f[g][table[3, tile]]

    def backward(g, source, base, tile):
        return nn(source[base + tile], tiles[tile]) + sums_b[g][table[7, HB + tile]]

    def hop_one(g):
        halo[g][0].wait()
        halo[g][1].wait()
        extras_b(g, hidden[g], HB)
        rims(g, rim_out[g])
        rim[g][0].start()
        rim[g][1].start()
        extras_f(g, hidden[g])

        def fwd_tile(tile, carry):
            fwd[g][HB + tile] = forward(g, hidden[g], tile).astype(BF16)
            return carry

        def fwd_rim(tile, carry):
            return fwd_tile(RT - HB + tile, fwd_tile(tile, carry))

        lax.fori_loop(0, HB, fwd_rim, 0, unroll=HB)
        edge[g][0].start()
        edge[g][1].start()

        def inner(tile, carry):
            bwd[g][tile] = backward(g, hidden[g], HB, tile).astype(BF16)
            return fwd_tile(tile, carry)

        lax.fori_loop(HB, RT - HB, inner, 0, unroll=INNER)

    def backward_two(g):
        rim[g][0].wait()
        rim[g][1].wait()

        def bwd_rim(tile, carry):
            low, high = tile, RT - HB + tile
            bwd[g][low] = (
                backward(g, hidden[g], HB, low) + rim_in[g][tile].astype(F32)
            ).astype(BF16)
            bwd[g][high] = (
                backward(g, hidden[g], HB, high) + rim_in[g][HB + tile].astype(F32)
            ).astype(BF16)
            return carry

        lax.fori_loop(0, HB, bwd_rim, 0, unroll=HB)
        extras_b(g, bwd[g], 0)
        rims(g, rim_out2[g])
        rim2[g][0].start()
        rim2[g][1].start()

    def mixed(g, first, received):
        columns_of_tiles = []
        for tile in range(PAIR):
            at = first + tile
            two = backward(g, bwd[g], 0, at)
            if received is not None:
                two = two + rim_in2[g][received + tile].astype(F32)
            columns_of_tiles.append(
                jnp.concatenate(
                    [
                        hidden[g][HB + at],
                        fwd[g][HB + at],
                        forward(g, fwd[g], at).astype(BF16),
                        bwd[g][at],
                        two.astype(BF16),
                    ],
                    axis=0,
                )
            )
        blocks = jnp.concatenate(columns_of_tiles, axis=1)
        rows_here = pl.ds(g * ROWS, ROWS)
        where = pl.ds(pl.multiple_of(first * T, PAIR * T), PAIR * T)
        total = nn(mix_w[...], blocks) + cur[rows_here, where].astype(F32) + bias_mix
        out[rows_here, where] = total.astype(BF16)

    def store(g, first, count, index):
        where = (pl.ds(g * ROWS, ROWS), pl.ds(first * T, count * T))
        return pltpu.make_async_copy(out.at[where], out_ref.at[where], out_sem.at[3 * g + index])

    stores = []

    def mix_inner(g):
        edge[g][0].wait()
        edge[g][1].wait()
        extras_f(g, fwd[g])

        def step(index, carry):
            mixed(g, HB + index * PAIR, None)
            return carry

        count = (RT - 2 * HB) // PAIR
        lax.fori_loop(0, count, step, 0, unroll=MIXED)
        stores.append(store(g, HB, RT - 2 * HB, 0))
        stores[-1].start()

    def mix_rim(g):
        rim2[g][0].wait()
        rim2[g][1].wait()

        def step(index, carry):
            mixed(g, index * PAIR, index * PAIR)
            mixed(g, RT - HB + index * PAIR, HB + index * PAIR)
            return carry

        lax.fori_loop(0, HB // PAIR, step, 0, unroll=HB // PAIR)
        for first, index in ((0, 1), (RT - HB, 2)):
            stores.append(store(g, first, HB, index))
            stores[-1].start()

    outer_gates(0)

    lane = iota((1, T), 1)
    pad = jnp.zeros((1, T - SLOTS), I32)
    rows = jnp.concatenate([rows_ref[...], pad], axis=1)
    cols = jnp.concatenate([cols_ref[...], pad], axis=1)
    live = (lane >= RT) & (lane < count_ref[0])
    far = jnp.full((1, T), 2 * T, I32)
    perm_f, take_f, keep_f, last_f = segments(jnp.where(live, rows, far), cols)
    perm_b, take_b, keep_b, last_b = segments(jnp.where(live, cols, far), rows)
    table_v[...] = jnp.concatenate(
        [perm_f, take_f, keep_f, last_f, perm_b, take_b, keep_b, last_b], axis=0
    )
    to_scalars = pltpu.make_async_copy(table_v, table, local_sem.at[9])
    to_scalars.start()
    for g in range(GROUPS):
        sums_f[g][0] = jnp.zeros((ROWS, T), F32)
        sums_b[g][0] = jnp.zeros((ROWS, T), F32)

    loads[8].wait()

    def turn(slot, carry):
        tiles_t[slot] = tiles[slot].T
        return carry

    lax.fori_loop(0, SLOTS, turn, 0, unroll=16)
    to_scalars.wait()

    inner_gates(0)
    hop_one(0)
    if GROUPS == 2:
        outer_gates(1)
        backward_two(0)
        inner_gates(1)
        hop_one(1)
        mix_inner(0)
        backward_two(1)
        mix_rim(0)
        mix_inner(1)
        mix_rim(1)
    else:
        backward_two(0)
        mix_inner(0)
        mix_rim(0)

    for group in range(GROUPS):
        for chunk in range(CHUNKS):
            shift(group, chunk).wait_send()
    for copy in stores:
        copy.wait()


def body(
    signal,
    time_weight,
    time_bias,
    mix_weight,
    mix_bias,
    tile_values,
    tile_rows,
    tile_cols,
    tile_count,
):
    width = signal.shape[2]
    whole = DAYS * CH
    hbm = pl.BlockSpec(memory_space=pltpu.HBM)
    panel = pltpu.VMEM((whole, width), BF16)

    def each(*shape):
        return [pltpu.VMEM(*shape) for _ in range(GROUPS)]

    result = pl.pallas_call(
        kernel,
        out_shape=jax.ShapeDtypeStruct((whole, width), BF16),
        in_specs=[hbm] * 9,
        out_specs=pl.BlockSpec(memory_space=pl.ANY),
        scratch_shapes=[
            panel,
            panel,
            pltpu.VMEM((SLOTS, T, T), BF16),
            pltpu.VMEM((SLOTS, T, T), BF16),
            each((RT + 2 * HB, ROWS, T), BF16),
            each((RT + 2 * HB, ROWS, T), BF16),
            each((RT, ROWS, T), BF16),
            each((EXTRA + 1, ROWS, T), F32),
            each((EXTRA + 1, ROWS, T), F32),
            each((2 * HB, ROWS, T), BF16),
            each((2 * HB, ROWS, T), BF16),
            each((2 * HB, ROWS, T), BF16),
            each((2 * HB, ROWS, T), BF16),
            panel,
            pltpu.VMEM((2 * ROWS, 2 * ROWS), BF16),
            pltpu.VMEM((ROWS, 5 * ROWS), BF16),
            pltpu.VMEM((2, CH, 2 * CH), BF16),
            pltpu.VMEM((2 * CH,), F32),
            pltpu.VMEM((CH, 5 * CH), BF16),
            pltpu.VMEM((CH,), F32),
            pltpu.VMEM((1, SLOTS), I32),
            pltpu.VMEM((1, SLOTS), I32),
            pltpu.SMEM((1,), I32),
            pltpu.VMEM((8, T), I32),
            pltpu.SMEM((8, T), I32),
            pltpu.SemaphoreType.DMA((10,)),
            pltpu.SemaphoreType.DMA((GROUPS * CHUNKS,)),
            pltpu.SemaphoreType.DMA((GROUPS * CHUNKS,)),
            pltpu.SemaphoreType.DMA((8 * GROUPS,)),
            pltpu.SemaphoreType.DMA((8 * GROUPS,)),
            pltpu.SemaphoreType.DMA((3 * GROUPS,)),
        ],
        compiler_params=pltpu.CompilerParams(
            collective_id=0, has_side_effects=True, vmem_limit_bytes=56 * 2**20
        ),
    )(
        signal.reshape(whole, width),
        jnp.transpose(time_weight, (0, 2, 1)),
        time_bias,
        mix_weight,
        mix_bias,
        tile_values[0],
        tile_rows,
        tile_cols,
        tile_count,
    )
    return result.reshape(signal.shape)


def solution(mesh):
    placed = (
        P("tm", None, "region"),
        P(),
        P(),
        P(),
        P(),
        P("region", None, None, None),
        P("region", None),
        P("region", None),
        P("region"),
    )
    return jax.shard_map(
        body, mesh=mesh, in_specs=placed, out_specs=P("tm", None, "region"), check_vma=False
    )
```

time: 52.9 us -> 39.3 us (0.74)
  Pallas kernels: 48.3 us -> 36.3 us
  local copies, waits for them, and re-layouts: 3.71 us -> 2.29 us
    pallas_call x1, Pallas kernels: 48.3 us -> 36.3 us  [body(): pl.pallas_call(kernel, out_shape=jax.ShapeDtypeStruct((whole, width), BF1...]
    unnamed x2 -> x1, local copies, waits for them, and re-layouts: 3.71 us -> 2.29 us
where the time goes in v2:
time: 39.3 us; the launch traced here: 39.2 us
  Pallas kernels  36.3 us (92%)
  local copies, waits for them, and re-layouts  2.29 us (6%)
  between operations  0.66 us (2%)
    pallas_call x1, Pallas kernels, body(): pl.pallas_call(kernel, out_shape=jax.ShapeDtypeStruct((whole, width), BF1...  36.3 us
    unnamed x1, local copies, waits for them, and re-layouts  2.29 us

profile of v2, /device:TPU:0, one launch (start us, length us, event | category | flops | bytes accessed | tf_op | source)
XLA Modules:
  0.0 39.2 jit_solution(14759694682312290877)
XLA Ops:
  0.7 36.3 %shard_map.91 = bf16[128,4096]{1,0:T(8,128)(2,1)} custom-call(bf16[128,4096]{1,0:T(8,128)(2,1)} %bitcast.6, bf16[2,32,64]{2,1,0:T(8,128)(2,1)} %bitcast.7, f32[64]{0:T(128)} %time_bias_hbm.1, bf16[32,160]{1,0:T(8,128)(2,1)} %mix_weight_hbm.1, f32[32]{0:T(128)} %mix_bias_hbm.1, bf16[96,128,128]{2,1,0:T(8,128)(2,1)} %bitcast.5, s32[1,96]{1,0:T(1,128)} %rows_hbm.1, ...), custom_call_target="tpu_custom_call" | custom-call | tf_op jit(solution)/shard_map/pallas_call | solution.py:468
  36.9 2.3 %copy.12 = bf16[4,32,4096]{2,1,0:T(8,128)(2,1)} copy(bf16[4,32,4096]{2,1,0:T(8,128)(2,1)} %bitcast.4) | data formatting | bytes 2097152

commit v3 on v2

--- a/solution.py
+++ b/solution.py
@@ -14,7 +14,7 @@
 SLOTS = 96
 RT = 32
 EXTRA = SLOTS - RT
-CHUNK = 8 if GROUPS == 2 else 4
+CHUNK = 4
 PAIR = 2
 UNROLL = 64
 INNER = 12
@@ -103,14 +103,22 @@
     tm = lax.axis_index("tm")
     regions = lax.axis_size("region")
     tms = lax.axis_size("tm")
-    above = (lax.rem(region + 1, regions), tm)
-    below = (lax.rem(region + regions - 1, regions), tm)
-    later = (region, lax.rem(tm + 1, tms))
-    earlier = (region, lax.rem(tm + tms - 1, tms))
+    above, below = (region + 1, tm), (region - 1, tm)
+    later, earlier = (region, tm + 1), (region, tm - 1)
+    has_above, has_below = region < regions - 1, region > 0
+    has_later, has_earlier = tm < tms - 1, tm > 0
 
     barrier = pltpu.get_barrier_semaphore()
-    for peer in (later, earlier, above, below):
-        pl.semaphore_signal(barrier, inc=1, device_id=peer, device_id_type=MESH)
+    for there, peer in (
+        (has_later, later),
+        (has_earlier, earlier),
+        (has_above, above),
+        (has_below, below),
+    ):
+
+        @pl.when(there)
+        def _(peer=peer):
+            pl.semaphore_signal(barrier, inc=1, device_id=peer, device_id_type=MESH)
 
     loads = [
         pltpu.make_async_copy(src, dst, local_sem.at[index])
@@ -130,7 +138,10 @@
     ]
     for load in loads:
         load.start()
-    pl.semaphore_wait(barrier, 4)
+    peers = sum(
+        there.astype(I32) for there in (has_later, has_earlier, has_above, has_below)
+    )
+    pl.semaphore_wait(barrier, peers)
 
     def columns(chunk):
         return pl.ds(chunk * (CHUNK * T), CHUNK * T)
@@ -148,15 +159,39 @@
         )
 
     order = [0, CHUNKS - 1] + list(range(1, CHUNKS - 1))
-    for group in range(GROUPS):
-        for chunk in order:
-            shift(group, chunk).start()
+
+    @pl.when(has_later)
+    def _():
+        for group in range(GROUPS):
+            for chunk in order:
+                shift(group, chunk).start()
+
+    @pl.when(jnp.logical_not(has_earlier))
+    def _():
+        lag[...] = jnp.zeros(lag.shape, BF16)
+
+    @pl.when(jnp.logical_not(has_below))
+    def _():
+        for g in range(GROUPS):
+            for ref, first in ((hidden[g], 0), (fwd[g], 0), (rim_in[g], 0), (rim_in2[g], 0)):
+                ref[first : first + HB] = jnp.zeros((HB, ROWS, T), BF16)
+
+    @pl.when(jnp.logical_not(has_above))
+    def _():
+        for g in range(GROUPS):
+            for ref, first in (
+                (hidden[g], HB + RT),
+                (fwd[g], HB + RT),
+                (rim_in[g], HB),
+                (rim_in2[g], HB),
+            ):
+                ref[first : first + HB] = jnp.zeros((HB, ROWS, T), BF16)
+
     for load in loads[:7]:
         load.wait()
 
     spread = (lax.rem(iota((ROWS, CH), 0), CH) == iota((ROWS, CH), 1)).astype(BF16)
     same_day = iota((ROWS, ROWS), 0) // CH == iota((ROWS, ROWS), 1) // CH
-    has_earlier = jnp.where(tm == 0, 0.0, 1.0)
     for part in range(2):
         tall = [nn(spread, time_weight_ref[tap]).astype(BF16) for tap in range(2)]
         pick = (
@@ -164,8 +199,6 @@
         ).astype(BF16)
         for tap in range(2):
             wide = nn(tall[tap], pick).T * (1.0 if part == 0 else 0.5)
-            if tap == 0:
-                wide = wide * has_earlier
             conv_w[part * ROWS : (part + 1) * ROWS, tap * ROWS : (tap + 1) * ROWS] = jnp.where(
                 same_day, wide, 0.0
             ).astype(BF16)
@@ -200,6 +233,20 @@
             device_id_type=MESH,
         )
 
+    def start_low(pair):
+        pl.when(has_below)(pair[0].start)
+
+    def start_high(pair):
+        pl.when(has_above)(pair[1].start)
+
+    def receive(pair):
+        pl.when(has_above)(pair[0].wait_recv)
+        pl.when(has_below)(pair[1].wait_recv)
+
+    def sent(pair):
+        pl.when(has_below)(pair[0].wait_send)
+        pl.when(has_above)(pair[1].wait_send)
+
     first_tiles, last_tiles = pl.ds(HB, HB), pl.ds(RT, HB)
     from_below, from_above = pl.ds(0, HB), pl.ds(HB + RT, HB)
     rim_first, rim_last = pl.ds(0, HB), pl.ds(HB, HB)
@@ -232,7 +279,10 @@
         )
 
     def gate(group, chunk):
-        shift(group, chunk).wait_recv()
+        @pl.when(has_earlier)
+        def _():
+            shift(group, chunk).wait_recv()
+
         rows_here = pl.ds(group * ROWS, ROWS)
 
         def part(index, carry):
@@ -252,9 +302,9 @@
 
     def outer_gates(group):
         gate(group, 0)
-        halo[group][0].start()
+        start_low(halo[group])
         gate(group, CHUNKS - 1)
-        halo[group][1].start()
+        start_high(halo[group])
 
     def inner_gates(group):
         for chunk in range(1, CHUNKS - 1):
@@ -290,12 +340,11 @@
         return nn(source[base + tile], tiles[tile]) + sums_b[g][table[7, HB + tile]]
 
     def hop_one(g):
-        halo[g][0].wait()
-        halo[g][1].wait()
+        receive(halo[g])
         extras_b(g, hidden[g], HB)
         rims(g, rim_out[g])
-        rim[g][0].start()
-        rim[g][1].start()
+        start_low(rim[g])
+        start_high(rim[g])
         extras_f(g, hidden[g])
 
         def fwd_tile(tile, carry):
@@ -306,8 +355,8 @@
             return fwd_tile(RT - HB + tile, fwd_tile(tile, carry))
 
         lax.fori_loop(0, HB, fwd_rim, 0, unroll=HB)
-        edge[g][0].start()
-        edge[g][1].start()
+        start_low(edge[g])
+        start_high(edge[g])
 
         def inner(tile, carry):
             bwd[g][tile] = backward(g, hidden[g], HB, tile).astype(BF16)
@@ -316,8 +365,7 @@
         lax.fori_loop(HB, RT - HB, inner, 0, unroll=INNER)
 
     def backward_two(g):
-        rim[g][0].wait()
-        rim[g][1].wait()
+        receive(rim[g])
 
         def bwd_rim(tile, carry):
             low, high = tile, RT - HB + tile
@@ -332,8 +380,8 @@
         lax.fori_loop(0, HB, bwd_rim, 0, unroll=HB)
         extras_b(g, bwd[g], 0)
         rims(g, rim_out2[g])
-        rim2[g][0].start()
-        rim2[g][1].start()
+        start_low(rim2[g])
+        start_high(rim2[g])
 
     def mixed(g, first, received):
         columns_of_tiles = []
@@ -367,8 +415,7 @@
     stores = []
 
     def mix_inner(g):
-        edge[g][0].wait()
-        edge[g][1].wait()
+        receive(edge[g])
         extras_f(g, fwd[g])
 
         def step(index, carry):
@@ -381,8 +428,7 @@
         stores[-1].start()
 
     def mix_rim(g):
-        rim2[g][0].wait()
-        rim2[g][1].wait()
+        receive(rim2[g])
 
         def step(index, carry):
             mixed(g, index * PAIR, index * PAIR)
@@ -424,24 +470,19 @@
 
     inner_gates(0)
     hop_one(0)
-    if GROUPS == 2:
-        outer_gates(1)
-        backward_two(0)
-        inner_gates(1)
-        hop_one(1)
-        mix_inner(0)
-        backward_two(1)
-        mix_rim(0)
-        mix_inner(1)
-        mix_rim(1)
-    else:
-        backward_two(0)
-        mix_inner(0)
-        mix_rim(0)
+    backward_two(0)
+    mix_inner(0)
+    mix_rim(0)
+
+    @pl.when(has_later)
+    def _():
+        for group in range(GROUPS):
+            for chunk in range(CHUNKS):
+                shift(group, chunk).wait_send()
 
     for group in range(GROUPS):
-        for chunk in range(CHUNKS):
-            shift(group, chunk).wait_send()
+        for pair in (halo[group], rim[group], edge[group], rim2[group]):
+            sent(pair)
     for copy in stores:
         copy.wait()
 

time: 39.3 us -> 33.9 us (0.86)
  the two profiles are of different devices: /device:TPU:0 before, /device:TPU:126 now
where the time goes in v3:
time: 33.9 us; the launch traced here: 33.8 us
  Pallas kernels  30.8 us (91%)
  local copies, waits for them, and re-layouts  2.29 us (7%)
  between operations  0.66 us (2%)
    pallas_call x1, Pallas kernels, body(): pl.pallas_call(kernel, out_shape=jax.ShapeDtypeStruct((whole, width), BF1...  30.8 us
    unnamed x1, local copies, waits for them, and re-layouts  2.29 us

profile of v3, /device:TPU:126, one launch (start us, length us, event | category | flops | bytes accessed | tf_op | source)
XLA Modules:
  0.0 33.8 jit_solution(9538219359494880532)
XLA Ops:
  0.7 30.8 %shard_map.91 = bf16[128,4096]{1,0:T(8,128)(2,1)} custom-call(bf16[128,4096]{1,0:T(8,128)(2,1)} %bitcast.6, bf16[2,32,64]{2,1,0:T(8,128)(2,1)} %bitcast.7, f32[64]{0:T(128)} %time_bias_hbm.1, bf16[32,160]{1,0:T(8,128)(2,1)} %mix_weight_hbm.1, f32[32]{0:T(128)} %mix_bias_hbm.1, bf16[96,128,128]{2,1,0:T(8,128)(2,1)} %bitcast.5, s32[1,96]{1,0:T(1,128)} %rows_hbm.1, ...), custom_call_target="tpu_custom_call" | custom-call | tf_op jit(solution)/shard_map/pallas_call | solution.py:509
  31.5 2.3 %copy.12 = bf16[4,32,4096]{2,1,0:T(8,128)(2,1)} copy(bf16[4,32,4096]{2,1,0:T(8,128)(2,1)} %bitcast.4) | data formatting | bytes 2097152

commit v4 on v3

--- a/solution.py
+++ b/solution.py
@@ -16,6 +16,8 @@
 EXTRA = SLOTS - RT
 CHUNK = 4
 PAIR = 2
+HALVES = 2
+HALF = ROWS // HALVES
 UNROLL = 64
 INNER = 12
 MIXED = 4
@@ -136,7 +138,7 @@
             ]
         )
     ]
-    for load in loads:
+    for load in loads[:7]:
         load.start()
     peers = sum(
         there.astype(I32) for there in (has_later, has_earlier, has_above, has_below)
@@ -187,6 +189,8 @@
             ):
                 ref[first : first + HB] = jnp.zeros((HB, ROWS, T), BF16)
 
+    for load in loads[7:]:
+        load.start()
     for load in loads[:7]:
         load.wait()
 
@@ -247,12 +251,15 @@
         pl.when(has_below)(pair[0].wait_send)
         pl.when(has_above)(pair[1].wait_send)
 
+    def half_rows(h):
+        return pl.ds(h * HALF, HALF)
+
     first_tiles, last_tiles = pl.ds(HB, HB), pl.ds(RT, HB)
     from_below, from_above = pl.ds(0, HB), pl.ds(HB + RT, HB)
     rim_first, rim_last = pl.ds(0, HB), pl.ds(HB, HB)
     halo, rim, edge, rim2 = [], [], [], []
     for g in range(GROUPS):
-        base = 8 * g
+        base = 12 * g
         halo.append(
             (
                 to_region(hidden[g].at[first_tiles], hidden[g].at[from_above], base, below),
@@ -260,10 +267,23 @@
             )
         )
         rim.append(
-            (
-                to_region(rim_out[g].at[rim_first], rim_in[g].at[rim_last], base + 2, below),
-                to_region(rim_out[g].at[rim_last], rim_in[g].at[rim_first], base + 3, above),
-            )
+            [
+                (
+                    to_region(
+                        rim_out[g].at[rim_first, half_rows(h)],
+                        rim_in[g].at[rim_last, half_rows(h)],
+                        base + 2 + 6 * h,
+                        below,
+                    ),
+                    to_region(
+                        rim_out[g].at[rim_last, half_rows(h)],
+                        rim_in[g].at[rim_first, half_rows(h)],
+                        base + 3 + 6 * h,
+                        above,
+                    ),
+                )
+                for h in range(HALVES)
+            ]
         )
         edge.append(
             (
@@ -272,10 +292,23 @@
             )
         )
         rim2.append(
-            (
-                to_region(rim_out2[g].at[rim_first], rim_in2[g].at[rim_last], base + 6, below),
-                to_region(rim_out2[g].at[rim_last], rim_in2[g].at[rim_first], base + 7, above),
-            )
+            [
+                (
+                    to_region(
+                        rim_out2[g].at[rim_first, half_rows(h)],
+                        rim_in2[g].at[rim_last, half_rows(h)],
+                        base + 6 + 4 * h,
+                        below,
+                    ),
+                    to_region(
+                        rim_out2[g].at[rim_last, half_rows(h)],
+                        rim_in2[g].at[rim_first, half_rows(h)],
+                        base + 7 + 4 * h,
+                        above,
+                    ),
+                )
+                for h in range(HALVES)
+            ]
         )
 
     def gate(group, chunk):
@@ -310,25 +343,31 @@
         for chunk in range(1, CHUNKS - 1):
             gate(group, chunk)
 
-    def extras(source, base, values, sums, first):
+    def extras(source, base, values, sums, first, start, count):
+        here = pl.ds(start, count)
+
         def add(place, running):
-            product = nn(source[table[first + 1, place] + base], values[table[first, place]])
+            product = nn(
+                source[table[first + 1, place] + base, here, :], values[table[first, place]]
+            )
             running = jnp.where(table[first + 2, place] > 0, running, 0.0) + product
-            sums[place + 1] = running
+            sums[place + 1, here, :] = running
             return running
 
-        lax.fori_loop(0, EXTRA, add, jnp.zeros((ROWS, T), F32), unroll=UNROLL)
+        lax.fori_loop(0, EXTRA, add, jnp.zeros((count, T), F32), unroll=UNROLL)
 
     def extras_f(g, source):
-        extras(source, 0, tiles_t, sums_f[g], 0)
-
-    def extras_b(g, source, base):
-        extras(source, base, tiles, sums_b[g], 4)
-
-    def rims(g, target):
+        extras(source, 0, tiles_t, sums_f[g], 0, 0, ROWS)
+
+    def extras_b(g, source, base, h):
+        extras(source, base, tiles, sums_b[g], 4, h * HALF, HALF)
+
+    def rims(g, target, h):
+        here = half_rows(h)
+
         def fill(tile, carry):
-            target[tile] = sums_b[g][table[7, tile]].astype(BF16)
-            target[HB + tile] = sums_b[g][table[7, HB + RT + tile]].astype(BF16)
+            target[tile, here, :] = sums_b[g][table[7, tile], here, :].astype(BF16)
+            target[HB + tile, here, :] = sums_b[g][table[7, HB + RT + tile], here, :].astype(BF16)
             return carry
 
         lax.fori_loop(0, HB, fill, 0, unroll=HB)
@@ -341,10 +380,11 @@
 
     def hop_one(g):
         receive(halo[g])
-        extras_b(g, hidden[g], HB)
-        rims(g, rim_out[g])
-        start_low(rim[g])
-        start_high(rim[g])
+        for h in range(HALVES):
+            extras_b(g, hidden[g], HB, h)
+            rims(g, rim_out[g], h)
+            start_low(rim[g][h])
+            start_high(rim[g][h])
         extras_f(g, hidden[g])
 
         def fwd_tile(tile, carry):
@@ -354,34 +394,34 @@
         def fwd_rim(tile, carry):
             return fwd_tile(RT - HB + tile, fwd_tile(tile, carry))
 
+
+        def inner(tile, carry):
+            bwd[g][tile] = backward(g, hidden[g], HB, tile).astype(BF16)
+            return fwd_tile(tile, carry)
+
+        lax.fori_loop(HB, RT - HB, inner, 0, unroll=INNER)
         lax.fori_loop(0, HB, fwd_rim, 0, unroll=HB)
         start_low(edge[g])
         start_high(edge[g])
 
-        def inner(tile, carry):
-            bwd[g][tile] = backward(g, hidden[g], HB, tile).astype(BF16)
-            return fwd_tile(tile, carry)
-
-        lax.fori_loop(HB, RT - HB, inner, 0, unroll=INNER)
-
     def backward_two(g):
-        receive(rim[g])
-
-        def bwd_rim(tile, carry):
-            low, high = tile, RT - HB + tile
-            bwd[g][low] = (
-                backward(g, hidden[g], HB, low) + rim_in[g][tile].astype(F32)
-            ).astype(BF16)
-            bwd[g][high] = (
-                backward(g, hidden[g], HB, high) + rim_in[g][HB + tile].astype(F32)
-            ).astype(BF16)
-            return carry
-
-        lax.fori_loop(0, HB, bwd_rim, 0, unroll=HB)
-        extras_b(g, bwd[g], 0)
-        rims(g, rim_out2[g])
-        start_low(rim2[g])
-        start_high(rim2[g])
+        for h in range(HALVES):
+            here = half_rows(h)
+            receive(rim[g][h])
+
+            def bwd_rim(tile, carry):
+                for at, arrived in ((tile, tile), (RT - HB + tile, HB + tile)):
+                    total = nn(hidden[g][HB + at, here, :], tiles[at])
+                    total = total + sums_b[g][table[7, HB + at], here, :]
+                    total = total + rim_in[g][arrived, here, :].astype(F32)
+                    bwd[g][at, here, :] = total.astype(BF16)
+                return carry
+
+            lax.fori_loop(0, HB, bwd_rim, 0, unroll=HB)
+            extras_b(g, bwd[g], 0, h)
+            rims(g, rim_out2[g], h)
+            start_low(rim2[g][h])
+            start_high(rim2[g][h])
 
     def mixed(g, first, received):
         columns_of_tiles = []
@@ -428,7 +468,8 @@
         stores[-1].start()
 
     def mix_rim(g):
-        receive(rim2[g])
+        for h in range(HALVES):
+            receive(rim2[g][h])
 
         def step(index, carry):
             mixed(g, index * PAIR, index * PAIR)
@@ -446,7 +487,7 @@
     pad = jnp.zeros((1, T - SLOTS), I32)
     rows = jnp.concatenate([rows_ref[...], pad], axis=1)
     cols = jnp.concatenate([cols_ref[...], pad], axis=1)
-    live = (lane >= RT) & (lane < count_ref[0])
+    live = (lane >= RT) & (lane < count_ref[...])
     far = jnp.full((1, T), 2 * T, I32)
     perm_f, take_f, keep_f, last_f = segments(jnp.where(live, rows, far), cols)
     perm_b, take_b, keep_b, last_b = segments(jnp.where(live, cols, far), rows)
@@ -481,7 +522,7 @@
                 shift(group, chunk).wait_send()
 
     for group in range(GROUPS):
-        for pair in (halo[group], rim[group], edge[group], rim2[group]):
+        for pair in (halo[group], edge[group], *rim[group], *rim2[group]):
             sent(pair)
     for copy in stores:
         copy.wait()
@@ -534,14 +575,14 @@
             pltpu.VMEM((CH,), F32),
             pltpu.VMEM((1, SLOTS), I32),
             pltpu.VMEM((1, SLOTS), I32),
-            pltpu.SMEM((1,), I32),
+            pltpu.VMEM((1, 1), I32),
             pltpu.VMEM((8, T), I32),
             pltpu.SMEM((8, T), I32),
             pltpu.SemaphoreType.DMA((10,)),
             pltpu.SemaphoreType.DMA((GROUPS * CHUNKS,)),
             pltpu.SemaphoreType.DMA((GROUPS * CHUNKS,)),
-            pltpu.SemaphoreType.DMA((8 * GROUPS,)),
-            pltpu.SemaphoreType.DMA((8 * GROUPS,)),
+            pltpu.SemaphoreType.DMA((12 * GROUPS,)),
+            pltpu.SemaphoreType.DMA((12 * GROUPS,)),
             pltpu.SemaphoreType.DMA((3 * GROUPS,)),
         ],
         compiler_params=pltpu.CompilerParams(
@@ -556,7 +597,7 @@
         tile_values[0],
         tile_rows,
         tile_cols,
-        tile_count,
+        tile_count.reshape(1, 1),
     )
     return result.reshape(signal.shape)
 

time: 33.9 us -> 33.2 us (0.979)
  Pallas kernels: 30.8 us -> 30 us
    pallas_call x1, Pallas kernels: 30.8 us -> 30 us  [body(): pl.pallas_call(kernel, out_shape=jax.ShapeDtypeStruct((whole, width), BF1...]
where the time goes in v4:
time: 33.2 us; the launch traced here: 33 us
  Pallas kernels  30 us (90%)
  local copies, waits for them, and re-layouts  2.29 us (7%)
  between operations  0.66 us (2%)
    pallas_call x1, Pallas kernels, body(): pl.pallas_call(kernel, out_shape=jax.ShapeDtypeStruct((whole, width), BF1...  30 us
    unnamed x1, local copies, waits for them, and re-layouts  2.29 us

profile of v4, /device:TPU:126, one launch (start us, length us, event | category | flops | bytes accessed | tf_op | source)
XLA Modules:
  0.0 33.0 jit_solution(13521664650364972927)
XLA Ops:
  0.7 30.0 %shard_map.91 = bf16[128,4096]{1,0:T(8,128)(2,1)} custom-call(bf16[128,4096]{1,0:T(8,128)(2,1)} %bitcast.8, bf16[2,32,64]{2,1,0:T(8,128)(2,1)} %bitcast.9, f32[64]{0:T(128)} %time_bias_hbm.1, bf16[32,160]{1,0:T(8,128)(2,1)} %mix_weight_hbm.1, f32[32]{0:T(128)} %mix_bias_hbm.1, bf16[96,128,128]{2,1,0:T(8,128)(2,1)} %bitcast.7, s32[1,96]{1,0:T(1,128)} %rows_hbm.1, ...), custom_call_target="tpu_custom_call" | custom-call | tf_op jit(solution)/shard_map/pallas_call | solution.py:550
  30.7 2.3 %copy.12 = bf16[4,32,4096]{2,1,0:T(8,128)(2,1)} copy(bf16[4,32,4096]{2,1,0:T(8,128)(2,1)} %bitcast.6) | data formatting | bytes 2097152

commit v5 on v4

--- a/solution.py
+++ b/solution.py
@@ -528,6 +528,25 @@
         copy.wait()
 
 
+def hand_over(source, target, buffer, in_sem, out_sem):
+    pieces = [pl.ds(index * 32, 32) for index in range(4)]
+    arrive = [
+        pltpu.make_async_copy(source.at[piece], buffer.at[piece], in_sem.at[index])
+        for index, piece in enumerate(pieces)
+    ]
+    leave = [
+        pltpu.make_async_copy(buffer.at[piece], target.at[piece], out_sem.at[index])
+        for index, piece in enumerate(pieces)
+    ]
+    for copy in arrive:
+        copy.start()
+    for first, second in zip(arrive, leave):
+        first.wait()
+        second.start()
+    for copy in leave:
+        copy.wait()
+
+
 def body(
     signal,
     time_weight,
@@ -599,6 +618,19 @@
         tile_cols,
         tile_count.reshape(1, 1),
     )
+    anywhere = pl.BlockSpec(memory_space=pl.ANY)
+    result = pl.pallas_call(
+        hand_over,
+        out_shape=jax.ShapeDtypeStruct((whole, width), BF16),
+        in_specs=[anywhere],
+        out_specs=anywhere,
+        scratch_shapes=[
+            panel,
+            pltpu.SemaphoreType.DMA((4,)),
+            pltpu.SemaphoreType.DMA((4,)),
+        ],
+        compiler_params=pltpu.CompilerParams(vmem_limit_bytes=56 * 2**20),
+    )(result)
     return result.reshape(signal.shape)
 
 

time: 33.2 us -> 32.8 us (0.988)
  local copies, waits for them, and re-layouts: 2.29 us -> 0 us
  Pallas kernels: 30 us -> 32 us
    unnamed x1 -> x0, local copies, waits for them, and re-layouts: 2.29 us -> none
    pallas_call x0 -> x1, Pallas kernels: none -> 1.98 us  [body(): pl.pallas_call(hand_over, out_shape=jax.ShapeDtypeStruct((whole, width),...]
where the time goes in v5:
time: 32.8 us; the launch traced here: 32.7 us
  Pallas kernels  32 us (98%)
  between operations  0.66 us (2%)
    pallas_call x1, Pallas kernels, body(): pl.pallas_call(kernel, out_shape=jax.ShapeDtypeStruct((whole, width), BF1...  30 us
    pallas_call x1, Pallas kernels, body(): pl.pallas_call(hand_over, out_shape=jax.ShapeDtypeStruct((whole, width),...  1.98 us

profile of v5, /device:TPU:126, one launch (start us, length us, event | category | flops | bytes accessed | tf_op | source)
XLA Modules:
  0.0 32.7 jit_solution(8303233067897821218)
XLA Ops:
  0.7 30.0 %shard_map.91.source = bf16[128,4096]{1,0:T(8,128)(2,1)} custom-call(bf16[128,4096]{1,0:T(8,128)(2,1)} %bitcast.7, bf16[2,32,64]{2,1,0:T(8,128)(2,1)} %bitcast.8, f32[64]{0:T(128)} %time_bias_hbm.1, bf16[32,160]{1,0:T(8,128)(2,1)} %mix_weight_hbm.1, f32[32]{0:T(128)} %mix_bias_hbm.1, bf16[96,128,128]{2,1,0:T(8,128)(2,1)} %bitcast.6, s32[1,96]{1,0:T(1,128)} %rows_hbm.1, ...), custom_call_target="tpu_custom_call" | custom-call | tf_op jit(solution)/shard_map/pallas_call | solution.py:569
  30.7 2.0 %shard_map.92 = bf16[128,4096]{1,0:T(8,128)(2,1)} custom-call(bf16[128,4096]{1,0:T(8,128)(2,1)} %shard_map.91.source), custom_call_target="tpu_custom_call" | custom-call | tf_op jit(solution)/shard_map/pallas_call | solution.py:622
